TPU v7x, 32 devices: a whole 2x2x4 slice. The times are simulated.
32 devices in a mesh: groups: 2 (over y), dom: 16 (over z, x, core).
Axes of the slice: x: 2, y: 2, z: 4, core: 2. Of those that a mesh axis runs over, the one named last changes fastest.
Arguments:
- nodes: float32 [65536, 128], P(('groups', 'dom')), parts along dimension 0, may hold values from -6 to 6
- edges: float32 [512, 4, 128], P(('groups', 'dom')), parts along dimension 0, may hold values from -6 to 6
- adjacency: int32 [512, 4], P(('groups', 'dom')), parts along dimension 0, may hold values from 0 to 19
- boundary: int32 [64, 2], P(('groups', 'dom')), parts along dimension 0, may hold values from 0 to 15
- assign: int32 [65536], P(('groups', 'dom')), parts along dimension 0, may hold values from 0 to 767
- coarse_adj: int32 [64, 4], P(('groups', 'dom')), parts along dimension 0, may hold values from 0 to 5
- coarse_edges: float32 [64, 4, 128], P(('groups', 'dom')), parts along dimension 0, may hold values from -6 to 6
- counts: int32 [32], P(('groups', 'dom')), parts along dimension 0, may hold values from 8 to 16
- targets: float32 [4, 65536], P(None, ('groups', 'dom')), parts along dimension 1, may hold values from -6 to 6
- w_send: float32 [3, 128, 128], replicated, may hold values from -0.5 to 0.5
- w_recv: float32 [3, 128, 128], replicated, may hold values from -0.5 to 0.5
- w_update: float32 [3, 128, 128], replicated, may hold values from -0.5 to 0.5
- w_edge: float32 [3, 128], replicated, may hold values from -6 to 6
- bias: float32 [3, 128], replicated, may hold values from -3 to 3
- w_out: float32 [4, 128], replicated, may hold values from -0.5 to 0.5
Outputs:
- loss: float32 [2], P('groups'), parts along dimension 0
- d_nodes: float32 [65536, 128], P(('groups', 'dom')), parts along dimension 0
- g_send: float32 [6, 128, 128], P('groups'), parts along dimension 0
- g_recv: float32 [6, 128, 128], P('groups'), parts along dimension 0
- g_update: float32 [6, 128, 128], P('groups'), parts along dimension 0
- g_edge: float32 [6, 128], P('groups'), parts along dimension 0
- g_bias: float32 [6, 128], P('groups'), parts along dimension 0
- g_out: float32 [8, 128], P('groups'), parts along dimension 0
There are 2 independent parts, one for each index of `groups`. A program takes and returns all parts, laid end to end along the dimension named above; an argument that names none is the same for every part. Nothing has to cross between parts.
Inputs may be any that keep to these rules, and one draw needn't show every extreme that they name: `adjacency`: indices into own blocks (16), then 2 from the lower partition, then 2 from the upper. `boundary`: local block indices.
All inputs are finite; a program needn't handle non-finite values.
Results may differ from a plain program's by a relative error of at most 0.0003.
Values sent between devices are 32-bit elements; how exact they have to be, the bound alone decides.
A program may use at most 128 MiB of HBM per device.

v0:
```python
import jax
import jax.numpy as jnp
from jax import lax
from jax.sharding import PartitionSpec as P

HIGH = lax.Precision.HIGHEST


def passed_along(value, axis, steps):
    count = lax.axis_size(axis)
    leading, last = (max(0, -steps), min(count, count - steps))
    return lax.ppermute(value, axis, [(source, source + steps) for source in range(leading, last)])


def neighbours(upward, downward):
    from_below = passed_along(upward, "dom", 1)
    from_above = passed_along(downward, "dom", -1)
    return (from_below, from_above)


def layer_forward(feats, adj, edge, out_up, out_down, w_s, w_r, w_u, w_e, b_l, mask):
    from_below, from_above = neighbours(out_up, out_down)
    ext = jnp.concatenate([feats, from_below, from_above], 0)
    neigh = ext[adj]
    own = jnp.einsum("nbh,hg->nbg", feats, w_s, precision=HIGH)
    pre = (
        own[:, None]
        + jnp.einsum("nkbh,hg->nkbg", neigh, w_r, precision=HIGH)
        + edge[..., None] * w_e
        + b_l
    )
    sigma = jax.nn.sigmoid(pre)
    agg = jnp.sum(pre * sigma, axis=1)
    result = feats + mask[:, None, None] * jnp.einsum("nbh,hg->nbg", agg, w_u, precision=HIGH)
    return (result, (feats, neigh, pre, sigma, agg))


def layer_backward(grad_out, saved, adj, edge, sends, w_s, w_r, w_u, mask):
    feats, neigh, pre, sigma, agg = saved
    blocks = feats.shape[0]
    width = sends.shape[1]
    update = mask[:, None, None] * grad_out
    g_u = jnp.einsum("nbh,nbg->hg", agg, update, precision=HIGH)
    grad_agg = jnp.einsum("nbg,hg->nbh", update, w_u, precision=HIGH)
    grad_pre = grad_agg[:, None] * sigma * (1.0 + pre * (1.0 - sigma))
    g_b = jnp.sum(grad_pre, axis=(0, 1, 2))
    g_e = jnp.einsum("nkbh,nkb->h", grad_pre, edge, precision=HIGH)
    summed = jnp.sum(grad_pre, axis=1)
    g_s = jnp.einsum("nbh,nbg->hg", feats, summed, precision=HIGH)
    g_r = jnp.einsum("nkbh,nkbg->hg", neigh, grad_pre, precision=HIGH)
    grad_feats = grad_out + jnp.einsum("nbg,hg->nbh", summed, w_s, precision=HIGH)
    grad_neigh = jnp.einsum("nkbg,hg->nkbh", grad_pre, w_r, precision=HIGH)
    grad_ext = (
        jnp.zeros((blocks + 2 * width,) + feats.shape[1:], jnp.float32).at[adj].add(grad_neigh)
    )
    from_below, from_above = neighbours(
        grad_ext[blocks + width :], grad_ext[blocks : blocks + width]
    )
    grad_feats = grad_feats + grad_ext[:blocks]
    grad_feats = grad_feats.at[sends[1]].add(from_below).at[sends[0]].add(from_above)
    return (grad_feats, (g_s, g_r, g_u, g_e, g_b))


def local(
    nodes,
    edges,
    adjacency,
    boundary,
    assign,
    coarse_adj,
    coarse_edges,
    counts,
    targets,
    w_send,
    w_recv,
    w_update,
    w_edge,
    bias,
    w_out,
):
    blocks = edges.shape[0]
    size_b = edges.shape[2]
    width = nodes.shape[1]
    feats = nodes.reshape(blocks, size_b, width)
    mask = (jnp.arange(blocks, dtype=jnp.int32) < counts[0]).astype(jnp.float32)
    live_here = counts[0].astype(jnp.float32)
    scale = 1.0
    scale = 1.0 / (4.0 * size_b * lax.psum(live_here, "dom"))
    saves = []
    for level in range(2):
        feats, saved = layer_forward(
            feats,
            adjacency,
            edges,
            feats[boundary[0]],
            feats[boundary[1]],
            w_send[level],
            w_recv[level],
            w_update[level],
            w_edge[level],
            bias[level],
            mask,
        )
        saves.append(saved)
    flat = feats.reshape(blocks * size_b, width)
    ncd = flat.shape[0] // 8
    onehot = (assign[:, None] == jnp.arange(3 * ncd, dtype=jnp.int32)[None, :]).astype(jnp.float32)
    partial_sums = jnp.einsum("nc,nh->ch", onehot, flat, precision=HIGH)
    from_below, from_above = neighbours(partial_sums[2 * ncd :], partial_sums[ncd : 2 * ncd])
    coarse = (partial_sums[:ncd] + from_below + from_above) / 8.0
    cblocks = coarse_adj.shape[0]
    cfeat = coarse.reshape(cblocks, size_b, width)
    every = jnp.arange(cblocks, dtype=jnp.int32)
    csends = jnp.stack([every, every])
    cmask = jnp.ones((cblocks,), jnp.float32)
    cfeat, csaved = layer_forward(
        cfeat,
        coarse_adj,
        coarse_edges,
        cfeat,
        cfeat,
        w_send[2],
        w_recv[2],
        w_update[2],
        w_edge[2],
        bias[2],
        cmask,
    )
    cflat = cfeat.reshape(ncd, width)
    from_below, from_above = neighbours(cflat, cflat)
    cext = jnp.concatenate([cflat, from_below, from_above], 0)
    fine = flat + jnp.einsum("nc,ch->nh", onehot, cext, precision=HIGH)
    pred = jnp.einsum("oh,nh->on", w_out, fine, precision=HIGH)
    live = jnp.repeat(mask, size_b)
    error = pred - targets
    local_loss = jnp.sum(live * error * error)
    grad_pred = 2.0 * live * error * scale
    g_o = jnp.einsum("on,nh->oh", grad_pred, fine, precision=HIGH)
    readout = (g_o, local_loss, live_here)
    grad_fine = jnp.einsum("on,oh->nh", grad_pred, w_out, precision=HIGH)
    grad_cext = jnp.einsum("nc,nh->ch", onehot, grad_fine, precision=HIGH)
    from_below, from_above = neighbours(grad_cext[2 * ncd :], grad_cext[ncd : 2 * ncd])
    grad_coarse = grad_cext[:ncd] + from_below + from_above
    grad_cfeat, cgrads = layer_backward(
        grad_coarse.reshape(cblocks, size_b, width),
        csaved,
        coarse_adj,
        coarse_edges,
        csends,
        w_send[2],
        w_recv[2],
        w_update[2],
        cmask,
    )
    grad_cflat = grad_cfeat.reshape(ncd, width) / 8.0
    from_below, from_above = neighbours(grad_cflat, grad_cflat)
    grad_partial = jnp.concatenate([grad_cflat, from_below, from_above], 0)
    grad_flat = grad_fine + jnp.einsum("nc,ch->nh", onehot, grad_partial, precision=HIGH)
    grad_feats = grad_flat.reshape(blocks, size_b, width)
    fine_grads = [None, None]
    for level in (1, 0):
        grad_feats, grads = layer_backward(
            grad_feats,
            saves[level],
            adjacency,
            edges,
            boundary,
            w_send[level],
            w_recv[level],
            w_update[level],
            mask,
        )
        fine_grads[level] = grads
    merged = lax.psum(readout + cgrads + fine_grads[0] + fine_grads[1], "dom")
    readout = merged[0:3]
    cgrads = merged[3:8]
    fine_grads = [merged[8:13], merged[13:18]]
    g_o = readout[0]
    loss = readout[1]
    final_scale = 1.0 / (4.0 * size_b * readout[2])
    loss = loss * final_scale
    final_scale = 1.0
    ordered = [fine_grads[0], fine_grads[1], cgrads]
    stacks = [jnp.stack([group[item] for group in ordered]) * final_scale for item in range(5)]
    d_nodes = grad_feats.reshape(blocks * size_b, width) * final_scale
    return (
        loss.reshape(1),
        d_nodes,
        stacks[0],
        stacks[1],
        stacks[2],
        stacks[3],
        stacks[4],
        g_o * final_scale,
    )


def solution(mesh):
    in_specs = (
        P(("groups", "dom"), None),
        P(("groups", "dom"), None, None),
        P(("groups", "dom"), None),
        P(("groups", "dom"), None),
        P(("groups", "dom")),
        P(("groups", "dom"), None),
        P(("groups", "dom"), None, None),
        P(("groups", "dom")),
        P(None, ("groups", "dom")),
        P(),
        P(),
        P(),
        P(),
        P(),
        P(),
    )
    out_specs = (
        P("groups"),
        P(("groups", "dom"), None),
        P("groups", None, None),
        P("groups", None, None),
        P("groups", None, None),
        P("groups", None),
        P("groups", None),
        P("groups", None),
    )
    return jax.shard_map(local, mesh=mesh, in_specs=in_specs, out_specs=out_specs, check_vma=False)
```

profile of v0, /device:TPU:0, one launch (start us, length us, event | category | flops | bytes accessed | tf_op | source)
XLA Modules:
  0.0 379.6 jit_solution(3309946864714390105)
XLA Ops:
  8.0 1.8 gather_fusion
  9.8 2.4 collective-permute-start
  12.8 1.8 gather_fusion.1
  14.6 1.3 collective-permute-start.1
  17.2 2.2 fusion.92
  19.5 1.6 slice_bitcast_fusion
  22.0 1.4 pad_maximum_fusion
  23.4 2.8 gather_fusion.2
  26.2 7.9 %multiply_reduce_fusion.1 = (f32[16,128,128]{2,1,0:T(8,128)S(1)}, f32[16,4,128,128]{3,2,1,0:T(8,128)}) fusion(f32[128]{0:T(128)S(1)} %copy-done.42, f32[128]{0:T(128)S(1)} %copy-done.44, f32[16,4,128]{2,1,0:T(4,128)S(1)} %copy-done.24, f32[16,128,128]{2,1,0:T(8,128)S(1)} %fusion.92, f32[16,4,128,128]{3,2,1,0:T(8,128)} %bitcast.216, f32[3,128,128]{2,1,0:T(8,128)} %param.25), kind=kOutput, calls=%fused_computation.30 | convolution fusion | flops 1619787776 | bytes 10585088 | tf_op jit(solution)/shard_map/nkbh,hg->nkbg/dot_general | solution.py:28
  35.1 1.8 fusion.24
  38.3 5.1 %collective-permute-start.2 = (f32[2,128,128]{2,1,0:T(8,128)S(1)}, f32[2,128,128]{2,1,0:T(8,128)S(1)}, u32[]{:S(2)}, u32[]{:S(2)}) collective-permute-start(f32[2,128,128]{2,1,0:T(8,128)S(1)} %gather_fusion.3), channel_id=1, source_target_pairs={{0,1},{1,2},{2,3},{3,4},{4,5},{5,6},{6,7},{7,8},{8,9},{9,10},{10,1... | collective-permute-start | bytes 393224 | tf_op jit(solution)/shard_map/ppermute | solution.py:12
  43.4 1.5 collective-permute-start.3
  44.9 2.8 fusion.87
  48.0 2.8 gather_fusion.5
  50.8 7.8 %multiply_reduce_fusion = (f32[16,128,128]{2,1,0:T(8,128)S(1)}, f32[16,4,128,128]{3,2,1,0:T(8,128)}) fusion(f32[128]{0:T(128)S(1)} %copy-done.46, f32[128]{0:T(128)S(1)} %copy-done.48, f32[16,128,128]{2,1,0:T(8,128)} %fusion.87, f32[16,4,128]{2,1,0:T(4,128)S(1)} %copy-done.24, f32[16,4,128,128]{3,2,1,0:T(8,128)} %bitcast.218, f32[3,128,128]{2,1,0:T(8,128)} %param.25), kind=kOutput, calls=%fused_computation.27 | convolution fusion | flops 1619787776 | bytes 10585088 | tf_op jit(solution)/shard_map/nkbh,hg->nkbg/dot_general | solution.py:28
  59.7 5.4 %fusion.3 = f32[768,128]{1,0:T(8,128)S(1)} fusion(f32[2048,128]{1,0:T(8,128)S(1)} %bitcast.237, s32[2048]{0:T(1024)S(1)} %copy-done.54), kind=kOutput, calls=%fused_computation.20 | convolution fusion | flops 2417491968 | bytes 1449984 | tf_op jit(solution)/shard_map/nc,nh->ch/dot_general | solution.py:108
  65.1 5.5 %collective-permute-start.4 = (f32[256,128]{1,0:T(8,128)S(1)}, f32[256,128]{1,0:T(8,128)S(1)}, u32[]{:S(2)}, u32[]{:S(2)}) collective-permute-start(f32[256,128]{1,0:T(8,128)S(1)} %get-tuple-element.66), channel_id=1, source_target_pairs={{0,1},{1,2},{2,3},{3,4},{4,5},{5,6},{6,7},{7,8},{8,9},{9,10},{10,1... | collective-permute-start | bytes 393224 | tf_op jit(solution)/shard_map/ppermute | solution.py:12
  71.9 34.0 %psum.130 = f32[]{:T(128)} all-reduce(f32[]{:T(128)S(6)} %convert_element_type.12), channel_id=1, replica_groups=mesh['groups'=2,'dom'=16] {'dom'}, use_global_device_ids=true, to_apply=%region_5.0 | all-reduce | flops 1 | bytes 8 | tf_op jit(solution)/shard_map/psum | solution.py:174
  108.1 3.0 collective-permute-start.6
  112.9 1.6 multiply_reduce_fusion.2
  114.8 1.3 collective-permute-start.9
  116.1 3.7 collective-permute-start.8
  120.7 4.2 %fusion.18 = f32[2048,128]{1,0:T(8,128)S(1)} fusion(f32[2048,128]{1,0:T(8,128)} %bitcast.238, s32[2048]{0:T(1024)} %param.19, f32[256,128]{1,0:T(8,128)S(1)} %collective-permute-done.9, f32[256,128]{1,0:T(8,128)S(1)} %collective-permute-done.8, f32[256,128]{1,0:T(8,128)S(1)} %bitcast.244), kind=kOutput, calls=%fused_computation.43 | convolution fusion | flops 2417950720 | bytes 2498560 | tf_op jit(solution)/shard_map/nc,ch->nh/dot_general | solution.py:132
  125.0 2.4 fusion.112
  127.3 1.8 fusion.114
  129.2 5.4 %fusion.1 = f32[768,128]{1,0:T(8,128)S(1)} fusion(f32[2048,128]{1,0:T(8,128)S(1)} %fusion.114, s32[2048]{0:T(1024)S(1)} %copy-done.55), kind=kOutput, calls=%fused_computation.18 | convolution fusion | flops 2417491968 | bytes 1449984 | tf_op jit(solution)/shard_map/nc,nh->ch/dot_general | solution.py:141
  134.6 5.3 %collective-permute-start.10 = (f32[256,128]{1,0:T(8,128)S(1)}, f32[256,128]{1,0:T(8,128)S(1)}, u32[]{:S(2)}, u32[]{:S(2)}) collective-permute-start(f32[256,128]{1,0:T(8,128)S(1)} %get-tuple-element.64), channel_id=1, source_target_pairs={{0,1},{1,2},{2,3},{3,4},{4,5},{5,6},{6,7},{7,8},{8,9},{9,10},{10,1... | collective-permute-start | bytes 393224 | tf_op jit(solution)/shard_map/ppermute | solution.py:12
  139.9 1.5 collective-permute-start.11
  142.6 2.5 collective-permute-done.11
  149.2 2.2 fusion.73
  151.5 2.1 scatter_fusion
  153.6 1.9 fusion.25
  157.6 6.1 %collective-permute-start.12 = (f32[2,128,128]{2,1,0:T(8,128)S(1)}, f32[2,128,128]{2,1,0:T(8,128)S(1)}, u32[]{:S(2)}, u32[]{:S(2)}) collective-permute-start(f32[2,128,128]{2,1,0:T(8,128)S(1)} %get-tuple-element.63), channel_id=1, source_target_pairs={{0,1},{1,2},{2,3},{3,4},{4,5},{5,6},{6,7},{7,8},{8,9},{9,10},{10,1... | collective-permute-start | bytes 393224 | tf_op jit(solution)/shard_map/ppermute | solution.py:12
  163.6 1.6 convolution_bitcast_fusion.4
  165.3 2.1 scatter_fusion.1
  167.4 2.1 scatter_fusion.2
  171.7 5.9 %collective-permute-start.14 = (f32[256,128]{1,0:T(8,128)S(1)}, f32[256,128]{1,0:T(8,128)S(1)}, u32[]{:S(2)}, u32[]{:S(2)}) collective-permute-start(f32[256,128]{1,0:T(8,128)S(1)} %bitcast.246), channel_id=1, source_target_pairs={{0,1},{1,2},{2,3},{3,4},{4,5},{5,6},{6,7},{7,8},{8,9},{9,10},{10,1... | collective-permute-start | bytes 393224 | tf_op jit(solution)/shard_map/ppermute | solution.py:12
  178.6 4.4 %broadcast_multiply_fusion = (f32[2048,128]{1,0:T(8,128)S(1)}, f32[2048,128]{1,0:T(8,128)S(1)}) fusion(f32[2048]{0:T(1024)S(1)} %broadcast_bitcast_fusion, f32[2048,128]{1,0:T(8,128)} %copy-done.21, f32[256,128]{1,0:T(8,128)S(1)} %collective-permute-done.15, f32[256,128]{1,0:T(8,128)S(1)} %collective-permute-done.14, f32[256,128]{1,0:T(8,128)S(1)} %bitcast.247, ...), kind=kOutput, calls=%fused_computation.77 | convolution fusion | flops 2418212864 | bytes 3555328 | tf_op jit(solution)/shard_map/nc,ch->nh/dot_general | solution.py:158
  183.0 1.9 fusion.83
  185.0 2.6 fusion.127
  187.6 7.5 %fusion.31 = f32[1,128,128]{2,1,0:T(8,128)} fusion(f32[16,4,128,128]{3,2,1,0:T(8,128)S(1)} %get-tuple-element.56, f32[16,4,128,128]{3,2,1,0:T(8,128)S(1)} %bitcast.219), kind=kOutput, calls=%fused_computation.61 | convolution fusion | flops 1610612736 | bytes 8454144 | tf_op jit(solution)/shard_map/nkbh,nkbg->hg/dot_general | solution.py:50
  195.1 6.2 %fusion.69 = f32[16,4,128,128]{3,2,1,0:T(8,128)} fusion(f32[16,4,128,128]{3,2,1,0:T(8,128)S(1)} %get-tuple-element.56, f32[3,128,128]{2,1,0:T(8,128)} %param.25), kind=kOutput, calls=%fused_computation.110 | convolution fusion | flops 1610612736 | bytes 8454144 | tf_op jit(solution)/shard_map/nkbg,hg->nkbh/dot_general | solution.py:52
  201.3 2.5 convolution_bitcast_fusion.2
  203.9 2.5 convolution_bitcast_fusion.6
  206.5 8.8 %scatter_fusion.3 = f32[20,128,128]{2,1,0:T(8,128)S(1)} fusion(f32[20,128,128]{2,1,0:T(8,128)S(1)} %broadcast.95.clone, s32[64]{0:T(128)S(1)} %reshape.154, f32[64,128,128]{2,1,0:T(8,128)} %bitcast.221), kind=kCustom, calls=%fused_computation.10 | custom fusion | flops 1048576 | bytes 12583168 | tf_op jit(solution)/shard_map/scatter-add | solution.py:54
  215.3 2.7 fusion.22
  220.0 6.4 %collective-permute-start.16 = (f32[2,128,128]{2,1,0:T(8,128)S(1)}, f32[2,128,128]{2,1,0:T(8,128)S(1)}, u32[]{:S(2)}, u32[]{:S(2)}) collective-permute-start(f32[2,128,128]{2,1,0:T(8,128)S(1)} %get-tuple-element.61), channel_id=1, source_target_pairs={{0,1},{1,2},{2,3},{3,4},{4,5},{5,6},{6,7},{7,8},{8,9},{9,10},{10,1... | collective-permute-start | bytes 393224 | tf_op jit(solution)/shard_map/ppermute | solution.py:12
  226.5 2.3 fusion.39
  230.1 3.9 %convolution_bitcast_fusion.3 = f32[1,128,128]{2,1,0:T(8,128)} fusion(f32[16,128,128]{2,1,0:T(8,128)} %copy-done.13, f32[16,128,128]{2,1,0:T(8,128)S(1)} %scatter_fusion.5, f32[16]{0:T(128)S(1)} %copy-done.30), kind=kOutput, calls=%fused_computation.64 | convolution fusion | flops 402915328 | bytes 2162752 | tf_op jit(solution)/shard_map/nbh,nbg->hg/dot_general | solution.py:43
  234.0 1.9 fusion.44
  235.9 2.7 fusion.126
  238.7 7.5 %fusion.26 = f32[1,128,128]{2,1,0:T(8,128)} fusion(f32[16,4,128,128]{3,2,1,0:T(8,128)S(1)} %get-tuple-element.55, f32[16,4,128,128]{3,2,1,0:T(8,128)S(1)} %bitcast.217), kind=kOutput, calls=%fused_computation.60 | convolution fusion | flops 1610612736 | bytes 8454144 | tf_op jit(solution)/shard_map/nkbh,nkbg->hg/dot_general | solution.py:50
  246.2 2.3 fusion.36
  248.5 6.0 %fusion.65 = f32[16,4,128,128]{3,2,1,0:T(8,128)} fusion(f32[16,4,128,128]{3,2,1,0:T(8,128)S(1)} %get-tuple-element.55, f32[3,128,128]{2,1,0:T(8,128)} %param.25), kind=kOutput, calls=%fused_computation.106 | convolution fusion | flops 1610612736 | bytes 8454144 | tf_op jit(solution)/shard_map/nkbg,hg->nkbh/dot_general | solution.py:52
  254.6 2.5 convolution_bitcast_fusion.7
  257.2 8.8 %scatter_fusion.6 = f32[20,128,128]{2,1,0:T(8,128)S(1)} fusion(f32[20,128,128]{2,1,0:T(8,128)S(1)} %broadcast.95, s32[64]{0:T(128)S(1)} %reshape.154, f32[64,128,128]{2,1,0:T(8,128)} %bitcast.220), kind=kCustom, calls=%fused_computation.13 | custom fusion | flops 1048576 | bytes 12583168 | tf_op jit(solution)/shard_map/scatter-add | solution.py:54
  266.1 2.8 fusion.21
  270.2 5.6 %collective-permute-start.18 = (f32[2,128,128]{2,1,0:T(8,128)S(1)}, f32[2,128,128]{2,1,0:T(8,128)S(1)}, u32[]{:S(2)}, u32[]{:S(2)}) collective-permute-start(f32[2,128,128]{2,1,0:T(8,128)S(1)} %get-tuple-element.59), channel_id=1, source_target_pairs={{0,1},{1,2},{2,3},{3,4},{4,5},{5,6},{6,7},{7,8},{8,9},{9,10},{10,1... | collective-permute-start | bytes 393224 | tf_op jit(solution)/shard_map/ppermute | solution.py:12
  275.9 33.3 %all-reduce = (f32[]{:T(128)}, f32[1,128]{1,0:T(1,128)S(1)}, f32[1,128]{1,0:T(1,128)S(1)}, f32[1,128]{1,0:T(1,128)S(1)}, f32[1,128]{1,0:T(1,128)S(1)}, /*index=5...) all-reduce(f32[]{:T(128)} %get-tuple-element.82, ...), channel_id=1, replica_groups=mesh['groups'=2,'dom'=16] {'dom'}, use_global_device_ids=true, to_apply=%region_4.0 | all-reduce | flops 1281 | bytes 10248 | tf_op jit(solution)/shard_map/psum | solution.py:174
  311.1 2.1 scatter_fusion.7
  313.2 2.1 scatter_fusion.8
  315.3 51.2 %all-reduce.4.cloned.1.call-done = (f32[1,128,128]{1,2,0:T(8,128)}, f32[1,128,128]{1,2,0:T(8,128)}, f32[1,128,128]{1,2,0:T(8,128)}, f32[1,128,128]{2,1,0:T(8,128...) async-done(((f32[1,128,128]{1,2,0:T(8,128)}, f32[1,128,128]{1,2,0:T(8,128)}, ...) | async-done | bytes 589840 | tf_op jit(solution)/shard_map/psum | solution.py:174
  368.2 1.6 pad_maximum_fusion.4
  369.8 1.6 pad_maximum_fusion.5
  (185 shorter events, 30.6 us)
Async XLA Ops:
  7.2 117.8 %copy-start = (f32[4,128]{1,0:T(4,128)S(1)}, f32[4,128]{1,0:T(4,128)}, u32[]{:S(2)}) copy-start(f32[4,128]{1,0:T(4,128)} %param.29) | copy-start | bytes 6148
  7.2 359.3 %all-reduce.4.cloned.1.call-start = ((), (), s32[]{:S(2)}) async-start(), calls=%async_computation | async-start | bytes 1179648 | tf_op jit(solution)/shard_map/psum | solution.py:174
  9.8 12.2 %collective-permute-start = (f32[2,128,128]{2,1,0:T(8,128)S(1)}, f32[2,128,128]{2,1,0:T(8,128)S(1)}, u32[]{:S(2)}, u32[]{:S(2)}) collective-permute-start(f32[2,128,128]{2,1,0:T(8,128)S(1)} %gather_fusion), channel_id=1, source_target_pairs={{0,1},{1,2},{2,3},{3,4},{4,5},{5,6},{6,7},{7,8},{8,9},{9,10},{10,1... | collective-permute-start | bytes 393224 | tf_op jit(solution)/shard_map/ppermute | solution.py:12
  14.6 7.4 %collective-permute-start.1 = (f32[2,128,128]{2,1,0:T(8,128)S(1)}, f32[2,128,128]{2,1,0:T(8,128)S(1)}, u32[]{:S(2)}, u32[]{:S(2)}) collective-permute-start(f32[2,128,128]{2,1,0:T(8,128)S(1)} %gather_fusion.1), channel_id=1, source_target_pairs={{1,0},{2,1},{3,2},{4,3},{5,4},{6,5},{7,6},{8,7},{9,8},{10,9},{11,1... | collective-permute-start | bytes 393224 | tf_op jit(solution)/shard_map/ppermute | solution.py:12
  16.6 42.1 %copy-start.29 = (f32[16]{0:T(128)}, f32[16]{0:T(128)S(1)}, u32[]{:S(2)}) copy-start(f32[16]{0:T(128)S(1)} %compare_convert_fusion) | copy-start | bytes 196
  19.5 6.7 %copy-start.10 = (f32[16,128,128]{2,1,0:T(8,128)}, f32[16,128,128]{2,1,0:T(8,128)S(1)}, u32[]{:S(2)}) copy-start(f32[16,128,128]{2,1,0:T(8,128)S(1)} %fusion.92) | copy-start | bytes 3145732
  26.2 8.9 %copy-start.4 = (f32[2048,128]{1,0:T(8,128)S(1)}, f32[2048,128]{1,0:T(8,128)}, u32[]{:S(2)}) copy-start(f32[2048,128]{1,0:T(8,128)} %param.15) | copy-start | bytes 3145732
  38.3 9.4 %collective-permute-start.2 = (f32[2,128,128]{2,1,0:T(8,128)S(1)}, f32[2,128,128]{2,1,0:T(8,128)S(1)}, u32[]{:S(2)}, u32[]{:S(2)}) collective-permute-start(f32[2,128,128]{2,1,0:T(8,128)S(1)} %gather_fusion.3), channel_id=1, source_target_pairs={{0,1},{1,2},{2,3},{3,4},{4,5},{5,6},{6,7},{7,8},{8,9},{9,10},{10,1... | collective-permute-start | bytes 393224 | tf_op jit(solution)/shard_map/ppermute | solution.py:12
  43.4 4.5 %collective-permute-start.3 = (f32[2,128,128]{2,1,0:T(8,128)S(1)}, f32[2,128,128]{2,1,0:T(8,128)S(1)}, u32[]{:S(2)}, u32[]{:S(2)}) collective-permute-start(f32[2,128,128]{2,1,0:T(8,128)S(1)} %gather_fusion.4), channel_id=1, source_target_pairs={{1,0},{2,1},{3,2},{4,3},{5,4},{6,5},{7,6},{8,7},{9,8},{10,9},{11,1... | collective-permute-start | bytes 393224 | tf_op jit(solution)/shard_map/ppermute | solution.py:12
  50.8 7.8 %copy-start.23 = (f32[3,128,128]{2,1,0:T(8,128)S(1)}, f32[3,128,128]{2,1,0:T(8,128)}, u32[]{:S(2)}) copy-start(f32[3,128,128]{2,1,0:T(8,128)} %param.26) | copy-start | bytes 589828
  50.8 8.9 %copy-start.54 = (s32[2048]{0:T(1024)S(1)}, s32[2048]{0:T(1024)}, u32[]{:S(2)}) copy-start(s32[2048]{0:T(1024)} %param.19) | copy-start | bytes 24580
  58.6 6.5 %copy-start.14 = (f32[16,128,128]{2,1,0:T(8,128)}, f32[16,128,128]{2,1,0:T(8,128)S(1)}, u32[]{:S(2)}) copy-start(f32[16,128,128]{2,1,0:T(8,128)S(1)} %get-tuple-element.78) | copy-start | bytes 3145732
  58.6 13.3 %copy-start.53 = (s32[2,4]{1,0:T(2,128)S(1)}, s32[2,4]{1,0:T(2,128)}, u32[]{:S(2)}) copy-start(s32[2,4]{1,0:T(2,128)} %param.20) | copy-start | bytes 100
  59.7 5.5 %copy-start.22 = (f32[16,128,128]{2,1,0:T(8,128)}, f32[16,128,128]{2,1,0:T(8,128)S(1)}, u32[]{:S(2)}) copy-start(f32[16,128,128]{2,1,0:T(8,128)S(1)} %fusion.23) | copy-start | bytes 3145732
  59.7 53.2 %copy-start.31 = (f32[2,4,128]{2,1,0:T(4,128)S(1)}, f32[2,4,128]{2,1,0:T(4,128)}, u32[]{:S(2)}) copy-start(f32[2,4,128]{2,1,0:T(4,128)} %param.21) | copy-start | bytes 12292
  65.1 41.6 %collective-permute-start.4 = (f32[256,128]{1,0:T(8,128)S(1)}, f32[256,128]{1,0:T(8,128)S(1)}, u32[]{:S(2)}, u32[]{:S(2)}) collective-permute-start(f32[256,128]{1,0:T(8,128)S(1)} %get-tuple-element.66), channel_id=1, source_target_pairs={{0,1},{1,2},{2,3},{3,4},{4,5},{5,6},{6,7},{7,8},{8,9},{9,10},{10,1... | collective-permute-start | bytes 393224 | tf_op jit(solution)/shard_map/ppermute | solution.py:12
  70.6 36.1 %collective-permute-start.5 = (f32[256,128]{1,0:T(8,128)S(1)}, f32[256,128]{1,0:T(8,128)S(1)}, u32[]{:S(2)}, u32[]{:S(2)}) collective-permute-start(f32[256,128]{1,0:T(8,128)S(1)} %get-tuple-element.67), channel_id=1, source_target_pairs={{1,0},{2,1},{3,2},{4,3},{5,4},{6,5},{7,6},{8,7},{9,8},{10,9},{11,1... | collective-permute-start | bytes 393224 | tf_op jit(solution)/shard_map/ppermute | solution.py:12
  106.0 6.2 %copy-start.41 = (s32[8]{0:T(128)}, s32[8]{0:T(128)S(1)}, u32[]{:S(2)}) copy-start(s32[8]{0:T(128)S(1)} %reshape.186) | copy-start | bytes 100
  106.8 5.5 %collective-permute-start.7 = (f32[2,128,128]{2,1,0:T(8,128)S(1)}, f32[2,128,128]{2,1,0:T(8,128)S(1)}, u32[]{:S(2)}, u32[]{:S(2)}) collective-permute-start(f32[2,128,128]{2,1,0:T(8,128)S(1)} %bitcast.224), channel_id=1, source_target_pairs={{1,0},{2,1},{3,2},{4,3},{5,4},{6,5},{7,6},{8,7},{9,8},{10,9},{11,1... | collective-permute-start | bytes 393224 | tf_op jit(solution)/shard_map/ppermute | solution.py:12
  108.1 4.2 %collective-permute-start.6 = (f32[2,128,128]{2,1,0:T(8,128)S(1)}, f32[2,128,128]{2,1,0:T(8,128)S(1)}, u32[]{:S(2)}, u32[]{:S(2)}) collective-permute-start(f32[2,128,128]{2,1,0:T(8,128)S(1)} %bitcast.225), channel_id=1, source_target_pairs={{0,1},{1,2},{2,3},{3,4},{4,5},{5,6},{6,7},{7,8},{8,9},{9,10},{10,1... | collective-permute-start | bytes 393224 | tf_op jit(solution)/shard_map/ppermute | solution.py:12
  112.2 12.7 %copy-start.26 = (f32[2,128,128]{2,1,0:T(8,128)}, f32[2,128,128]{2,1,0:T(8,128)S(1)}, u32[]{:S(2)}) copy-start(f32[2,128,128]{2,1,0:T(8,128)S(1)} %fusion.81) | copy-start | bytes 393220
  112.9 14.4 %copy-start.28 = (f32[2048]{0:T(1024)S(1)}, f32[2048]{0:T(1024)}, u32[]{:S(2)}) copy-start(f32[2048]{0:T(1024)} %bitcast_multiply_fusion) | copy-start | bytes 24580
  112.9 16.3 %copy-start.55 = (s32[2048]{0:T(1024)S(1)}, s32[2048]{0:T(1024)}, u32[]{:S(2)}) copy-start(s32[2048]{0:T(1024)} %param.19) | copy-start | bytes 24580
  114.8 5.7 %collective-permute-start.9 = (f32[256,128]{1,0:T(8,128)S(1)}, f32[256,128]{1,0:T(8,128)S(1)}, u32[]{:S(2)}, u32[]{:S(2)}) collective-permute-start(f32[256,128]{1,0:T(8,128)S(1)} %bitcast.242), channel_id=1, source_target_pairs={{1,0},{2,1},{3,2},{4,3},{5,4},{6,5},{7,6},{8,7},{9,8},{10,9},{11,1... | collective-permute-start | bytes 393224 | tf_op jit(solution)/shard_map/ppermute | solution.py:12
  116.1 4.7 %collective-permute-start.8 = (f32[256,128]{1,0:T(8,128)S(1)}, f32[256,128]{1,0:T(8,128)S(1)}, u32[]{:S(2)}, u32[]{:S(2)}) collective-permute-start(f32[256,128]{1,0:T(8,128)S(1)} %bitcast.243), channel_id=1, source_target_pairs={{0,1},{1,2},{2,3},{3,4},{4,5},{5,6},{6,7},{7,8},{8,9},{9,10},{10,1... | collective-permute-start | bytes 393224 | tf_op jit(solution)/shard_map/ppermute | solution.py:12
  127.3 20.0 %copy-start.27 = (f32[2,128,128]{2,1,0:T(8,128)S(1)}, f32[2,128,128]{2,1,0:T(8,128)}, u32[]{:S(2)}) copy-start(f32[2,128,128]{2,1,0:T(8,128)} %copy-done.26) | copy-start | bytes 393220
  127.3 20.0 %copy-start.32 = (f32[2,4,128]{2,1,0:T(4,128)S(1)}, f32[2,4,128]{2,1,0:T(4,128)}, u32[]{:S(2)}) copy-start(f32[2,4,128]{2,1,0:T(4,128)} %param.21) | copy-start | bytes 12292
  127.3 20.0 %copy-start.50 = (f32[128]{0:T(128)S(1)}, f32[128]{0:T(128)}, u32[]{:S(2)}) copy-start(f32[128]{0:T(128)} %get-tuple-element.71) | copy-start | bytes 1540
  127.3 20.0 %copy-start.51 = (f32[128]{0:T(128)S(1)}, f32[128]{0:T(128)}, u32[]{:S(2)}) copy-start(f32[128]{0:T(128)} %get-tuple-element.88) | copy-start | bytes 1540
  129.2 19.0 %copy-start.21 = (f32[2048,128]{1,0:T(8,128)}, f32[2048,128]{1,0:T(8,128)S(1)}, u32[]{:S(2)}) copy-start(f32[2048,128]{1,0:T(8,128)S(1)} %fusion.114) | copy-start | bytes 3145732
  134.6 8.0 %collective-permute-start.10 = (f32[256,128]{1,0:T(8,128)S(1)}, f32[256,128]{1,0:T(8,128)S(1)}, u32[]{:S(2)}, u32[]{:S(2)}) collective-permute-start(f32[256,128]{1,0:T(8,128)S(1)} %get-tuple-element.64), channel_id=1, source_target_pairs={{0,1},{1,2},{2,3},{3,4},{4,5},{5,6},{6,7},{7,8},{8,9},{9,10},{10,1... | collective-permute-start | bytes 393224 | tf_op jit(solution)/shard_map/ppermute | solution.py:12
  139.9 5.2 %collective-permute-start.11 = (f32[256,128]{1,0:T(8,128)S(1)}, f32[256,128]{1,0:T(8,128)S(1)}, u32[]{:S(2)}, u32[]{:S(2)}) collective-permute-start(f32[256,128]{1,0:T(8,128)S(1)} %get-tuple-element.65), channel_id=1, source_target_pairs={{1,0},{2,1},{3,2},{4,3},{5,4},{6,5},{7,6},{8,7},{9,8},{10,9},{11,1... | collective-permute-start | bytes 393224 | tf_op jit(solution)/shard_map/ppermute | solution.py:12
  145.1 6.3 %copy-start.19 = (f32[256,128]{1,0:T(8,128)}, f32[256,128]{1,0:T(8,128)S(1)}, u32[]{:S(2)}) copy-start(f32[256,128]{1,0:T(8,128)S(1)} %fusion.62) | copy-start | bytes 393220
  146.2 31.4 %copy-start.33 = (f32[2,4,128]{2,1,0:T(4,128)S(1)}, f32[2,4,128]{2,1,0:T(4,128)}, u32[]{:S(2)}) copy-start(f32[2,4,128]{2,1,0:T(4,128)} %param.21) | copy-start | bytes 12292
  156.3 11.1 %collective-permute-start.13 = (f32[2,128,128]{2,1,0:T(8,128)}, f32[2,128,128]{2,1,0:T(8,128)S(1)}, u32[]{:S(2)}, u32[]{:S(2)}) collective-permute-start(f32[2,128,128]{2,1,0:T(8,128)} %get-tuple-element.62), channel_id=1, source_target_pairs={{1,0},{2,1},{3,2},{4,3},{5,4},{6,5},{7,6},{8,7},{9,8},{10,9},{11,1... | collective-permute-start | bytes 393224 | tf_op jit(solution)/shard_map/ppermute | solution.py:12
  157.6 7.7 %collective-permute-start.12 = (f32[2,128,128]{2,1,0:T(8,128)S(1)}, f32[2,128,128]{2,1,0:T(8,128)S(1)}, u32[]{:S(2)}, u32[]{:S(2)}) collective-permute-start(f32[2,128,128]{2,1,0:T(8,128)S(1)} %get-tuple-element.63), channel_id=1, source_target_pairs={{0,1},{1,2},{2,3},{3,4},{4,5},{5,6},{6,7},{7,8},{8,9},{9,10},{10,1... | collective-permute-start | bytes 393224 | tf_op jit(solution)/shard_map/ppermute | solution.py:12
  170.4 7.6 %collective-permute-start.15 = (f32[256,128]{1,0:T(8,128)S(1)}, f32[256,128]{1,0:T(8,128)S(1)}, u32[]{:S(2)}, u32[]{:S(2)}) collective-permute-start(f32[256,128]{1,0:T(8,128)S(1)} %bitcast.245), channel_id=1, source_target_pairs={{1,0},{2,1},{3,2},{4,3},{5,4},{6,5},{7,6},{8,7},{9,8},{10,9},{11,1... | collective-permute-start | bytes 393224 | tf_op jit(solution)/shard_map/ppermute | solution.py:12
  171.7 6.8 %collective-permute-start.14 = (f32[256,128]{1,0:T(8,128)S(1)}, f32[256,128]{1,0:T(8,128)S(1)}, u32[]{:S(2)}, u32[]{:S(2)}) collective-permute-start(f32[256,128]{1,0:T(8,128)S(1)} %bitcast.246), channel_id=1, source_target_pairs={{0,1},{1,2},{2,3},{3,4},{4,5},{5,6},{6,7},{7,8},{8,9},{9,10},{10,1... | collective-permute-start | bytes 393224 | tf_op jit(solution)/shard_map/ppermute | solution.py:12
  178.0 6.9 %copy-start.12 = (f32[16,128,128]{2,1,0:T(8,128)S(1)}, f32[16,128,128]{2,1,0:T(8,128)}, u32[]{:S(2)}) copy-start(f32[16,128,128]{2,1,0:T(8,128)} %fusion.87) | copy-start | bytes 3145732
  178.0 6.9 %copy-start.17 = (f32[16,4,128,128]{3,2,1,0:T(8,128)S(1)}, f32[16,4,128,128]{3,2,1,0:T(8,128)}, u32[]{:S(2)}) copy-start(f32[16,4,128,128]{3,2,1,0:T(8,128)} %get-tuple-element.79) | copy-start | bytes 12582916
  178.0 6.9 %copy-start.25 = (f32[16,4,128]{2,1,0:T(4,128)S(1)}, f32[16,4,128]{2,1,0:T(4,128)}, u32[]{:S(2)}) copy-start(f32[16,4,128]{2,1,0:T(4,128)} %param.16) | copy-start | bytes 98308
  178.0 6.9 %copy-start.47 = (f32[128]{0:T(128)S(1)}, f32[128]{0:T(128)}, u32[]{:S(2)}) copy-start(f32[128]{0:T(128)} %get-tuple-element.73) | copy-start | bytes 1540
  178.0 6.9 %copy-start.49 = (f32[128]{0:T(128)S(1)}, f32[128]{0:T(128)}, u32[]{:S(2)}) copy-start(f32[128]{0:T(128)} %get-tuple-element.86) | copy-start | bytes 1540
  183.0 18.3 %copy-start.18 = (f32[2048,128]{1,0:T(8,128)}, f32[2048,128]{1,0:T(8,128)S(1)}, u32[]{:S(2)}) copy-start(f32[2048,128]{1,0:T(8,128)S(1)} %get-tuple-element.85) | copy-start | bytes 3145732
  187.5 7.6 %copy-start.2 = (f32[16,4,128,128]{3,2,1,0:T(8,128)}, f32[16,4,128,128]{3,2,1,0:T(8,128)S(1)}, u32[]{:S(2)}) copy-start(f32[16,4,128,128]{3,2,1,0:T(8,128)S(1)} %get-tuple-element.56) | copy-start | bytes 12582916
  187.6 16.3 %copy-start.9 = (f32[16,128,128]{2,1,0:T(8,128)}, f32[16,128,128]{2,1,0:T(8,128)S(1)}, u32[]{:S(2)}) copy-start(f32[16,128,128]{2,1,0:T(8,128)S(1)} %get-tuple-element.35) | copy-start | bytes 3145732
  195.1 6.2 %copy-start.15 = (f32[16,128,128]{2,1,0:T(8,128)S(1)}, f32[16,128,128]{2,1,0:T(8,128)}, u32[]{:S(2)}) copy-start(f32[16,128,128]{2,1,0:T(8,128)} %copy-done.14) | copy-start | bytes 3145732
  195.1 6.2 %copy-start.30 = (f32[16]{0:T(128)S(1)}, f32[16]{0:T(128)}, u32[]{:S(2)}) copy-start(f32[16]{0:T(128)} %copy-done.29) | copy-start | bytes 196
  215.3 11.1 %copy-start.3 = (f32[16,4,128,128]{3,2,1,0:T(8,128)S(1)}, f32[16,4,128,128]{3,2,1,0:T(8,128)}, u32[]{:S(2)}) copy-start(f32[16,4,128,128]{3,2,1,0:T(8,128)} %copy-done.2) | copy-start | bytes 12582916
  215.3 13.5 %copy-start.37 = (s32[2]{0:T(128)S(1)}, s32[2]{0:T(128)}, u32[]{:S(2)}) copy-start(s32[2]{0:T(128)} %copy-done.36) | copy-start | bytes 28
  215.3 14.1 %copy-start.35 = (s32[2]{0:T(128)S(1)}, s32[2]{0:T(128)}, u32[]{:S(2)}) copy-start(s32[2]{0:T(128)} %copy-done.34) | copy-start | bytes 28
  218.7 10.7 %collective-permute-start.17 = (f32[2,128,128]{2,1,0:T(8,128)}, f32[2,128,128]{2,1,0:T(8,128)S(1)}, u32[]{:S(2)}, u32[]{:S(2)}) collective-permute-start(f32[2,128,128]{2,1,0:T(8,128)} %get-tuple-element.60), channel_id=1, source_target_pairs={{1,0},{2,1},{3,2},{4,3},{5,4},{6,5},{7,6},{8,7},{9,8},{10,9},{11,1... | collective-permute-start | bytes 393224 | tf_op jit(solution)/shard_map/ppermute | solution.py:12
  220.0 8.7 %collective-permute-start.16 = (f32[2,128,128]{2,1,0:T(8,128)S(1)}, f32[2,128,128]{2,1,0:T(8,128)S(1)}, u32[]{:S(2)}, u32[]{:S(2)}) collective-permute-start(f32[2,128,128]{2,1,0:T(8,128)S(1)} %get-tuple-element.61), channel_id=1, source_target_pairs={{0,1},{1,2},{2,3},{3,4},{4,5},{5,6},{6,7},{7,8},{8,9},{9,10},{10,1... | collective-permute-start | bytes 393224 | tf_op jit(solution)/shard_map/ppermute | solution.py:12
  226.4 9.4 %copy-start.11 = (f32[16,128,128]{2,1,0:T(8,128)S(1)}, f32[16,128,128]{2,1,0:T(8,128)}, u32[]{:S(2)}) copy-start(f32[16,128,128]{2,1,0:T(8,128)} %copy-done.10) | copy-start | bytes 3145732
  226.4 9.4 %copy-start.43 = (f32[128]{0:T(128)S(1)}, f32[128]{0:T(128)}, u32[]{:S(2)}) copy-start(f32[128]{0:T(128)} %get-tuple-element.72) | copy-start | bytes 1540
  226.4 9.4 %copy-start.45 = (f32[128]{0:T(128)S(1)}, f32[128]{0:T(128)}, u32[]{:S(2)}) copy-start(f32[128]{0:T(128)} %get-tuple-element.87) | copy-start | bytes 1540
  230.1 5.8 %copy-start.16 = (f32[16,4,128,128]{3,2,1,0:T(8,128)S(1)}, f32[16,4,128,128]{3,2,1,0:T(8,128)}, u32[]{:S(2)}) copy-start(f32[16,4,128,128]{3,2,1,0:T(8,128)} %get-tuple-element.77) | copy-start | bytes 12582916
  238.7 15.9 %copy-start.7 = (f32[16,128,128]{2,1,0:T(8,128)}, f32[16,128,128]{2,1,0:T(8,128)S(1)}, u32[]{:S(2)}) copy-start(f32[16,128,128]{2,1,0:T(8,128)S(1)} %get-tuple-element.33) | copy-start | bytes 3145732
  257.2 8.8 %copy-start.8 = (f32[16,128,128]{2,1,0:T(8,128)S(1)}, f32[16,128,128]{2,1,0:T(8,128)}, u32[]{:S(2)}) copy-start(f32[16,128,128]{2,1,0:T(8,128)} %copy-done.7) | copy-start | bytes 3145732
  257.2 114.2 %copy-start.1 = (f32[4,128]{1,0:T(4,128)S(1)}, f32[4,128]{1,0:T(4,128)}, u32[]{:S(2)}) copy-start(f32[4,128]{1,0:T(4,128)} %param.29) | copy-start | bytes 6148
  266.0 9.9 %copy-start.38 = (f32[4,128]{1,0:T(4,128)S(1)}, f32[4,128]{1,0:T(4,128)}, u32[]{:S(2)}) copy-start(f32[4,128]{1,0:T(4,128)} %fusion.113) | copy-start | bytes 6148
  266.0 9.9 %copy-start.52 = (f32[128]{0:T(128)S(1)}, f32[128]{0:T(128)}, u32[]{:S(2)}) copy-start(f32[128]{0:T(128)} %get-tuple-element.36) | copy-start | bytes 1540
  268.9 44.2 %collective-permute-start.19 = (f32[2,128,128]{2,1,0:T(8,128)S(1)}, f32[2,128,128]{2,1,0:T(8,128)S(1)}, u32[]{:S(2)}, u32[]{:S(2)}) collective-permute-start(f32[2,128,128]{2,1,0:T(8,128)S(1)} %get-tuple-element.58), channel_id=1, source_target_pairs={{1,0},{2,1},{3,2},{4,3},{5,4},{6,5},{7,6},{8,7},{9,8},{10,9},{11,1... | collective-permute-start | bytes 393224 | tf_op jit(solution)/shard_map/ppermute | solution.py:12
  270.2 40.8 %collective-permute-start.18 = (f32[2,128,128]{2,1,0:T(8,128)S(1)}, f32[2,128,128]{2,1,0:T(8,128)S(1)}, u32[]{:S(2)}, u32[]{:S(2)}) collective-permute-start(f32[2,128,128]{2,1,0:T(8,128)S(1)} %get-tuple-element.59), channel_id=1, source_target_pairs={{0,1},{1,2},{2,3},{3,4},{4,5},{5,6},{6,7},{7,8},{8,9},{9,10},{10,1... | collective-permute-start | bytes 393224 | tf_op jit(solution)/shard_map/ppermute | solution.py:12
  (13 other events, 36.9 us)
Sparse Core Ops, SparseCore 0:
  269.0 97.3 all-reduce.3
where the time goes:
time: 386 us; the launch traced here: 380 us
  matrix products  113 us (29%)
  blocking collectives  67.3 us (17%)
  starting transfers between devices  62.3 us (16%)
  waiting for transfers between devices  54.7 us (14%)
  other arithmetic  45.5 us (12%)
  between operations  18.6 us (5%)
  local copies, waits for them, and re-layouts  18 us (5%)
    psum x2, blocking collectives, local(): merged = lax.psum(readout + cgrads + fine_grads[0] + fine_grads[1], 'dom')  67.3 us
    ppermute x20, starting transfers between devices, passed_along(): lax.ppermute(value, axis, [(source, source + steps) for source in range(l...  62.2 us
    psum x1, waiting for transfers between devices, local(): merged = lax.psum(readout + cgrads + fine_grads[0] + fine_grads[1], 'dom')  51.2 us
    scatter-add x3, other arithmetic, layer_backward(): jnp.zeros((blocks + 2 * width,) + feats.shape[1:], jnp.float32).at[adj]  19.7 us
    dot_general x3, matrix products, layer_forward(): jnp.einsum('nkbh,hg->nkbg', neigh, w_r, precision=HIGH)  17.3 us
    dot_general x3, matrix products, layer_backward(): g_r = jnp.einsum('nkbh,nkbg->hg', neigh, grad_pre, precision=HIGH)  16.7 us
    dot_general x3, matrix products, layer_backward(): grad_neigh = jnp.einsum('nkbg,hg->nkbh', grad_pre, w_r, precision=HIGH)  14.5 us
    scatter-add x6, other arithmetic, layer_backward(): grad_feats.at[sends[1]].add(from_below).at[sends[0]].add(from_above)  9.72 us
  transfers between devices with their start and end apart: 21, of which 5 were waited for; matrix products, arithmetic and copies ran while one was open for 7% of the time, Pallas kernels for 0%

commit v1 on v0

v1 whole, which is shorter than its diff:
```python
import functools

import jax
import jax.numpy as jnp
from jax import lax
from jax.experimental import pallas as pl
from jax.experimental.pallas import tpu as pltpu
from jax.sharding import PartitionSpec as P

F32 = jnp.float32
BF16 = jnp.bfloat16
W = 128


def split(x):
    hi = x.astype(BF16)
    lo = (x - hi.astype(F32)).astype(BF16)
    return hi, lo


def stacked(x):
    return jnp.concatenate(split(x), axis=0)


def doubled(w):
    hi, lo = split(w)
    return jnp.concatenate([jnp.concatenate([hi, hi], 1), jnp.concatenate([lo, lo], 1)], 0)


def dot(a, b):
    return lax.dot_general(a, b, (((1,), (0,)), ((), ())), preferred_element_type=F32)


def dot_t(a, b):
    return lax.dot_general(a, b, (((1,), (1,)), ((), ())), preferred_element_type=F32)


def halves(r):
    m = r.shape[0] // 2
    return r[:m] + r[m:]


def quads(r):
    r = halves(r)
    return r[:, :W] + r[:, W:]


def group(ref, i, g):
    return jnp.concatenate([ref[g * i + j] for j in range(g)], axis=1) if g > 1 else ref[i]


def cols(x, j):
    return x[:, j * W:(j + 1) * W]


def kernel(N, nb, nc, K, KC, R, off,
           meta, nodes, edges, assign, cedges, targets, ws, wr, wu, we, bias, wo,
           dn, gs_o, gr_o, gu_o, ge_o, gb_o, go_o, loss_o,
           h0, h1, h2, c0, c1, own, recv, D0, D1, D2, agg0, agg1, agg2, G, S, gr, gc,
           oh, h2s, WF, WU, WUb, WSb, WRb, WE, BI, eacc, bacc, xb, st, xs, sts, t8, w8, gp, acc, rsb, res,
           ssem, rsem, sssem, srsem, assem, arsem):
    me = lax.axis_index("dom")
    steps = N.bit_length() - 1
    n = nb * W
    ncd = nc * W
    up_ok = me < N - 1
    down_ok = me > 0

    def partner(s):
        bit = 1 << s
        return me + bit * (1 - 2 * ((me // bit) % 2))

    def dev(d):
        return {"dom": d}

    MESH = pl.DeviceIdType.MESH

    @pl.when(me == 0)
    def _():
        for x in range(8):
            xb[x, 0:2] = jnp.zeros((2, W, W), F32)
        for x in range(2):
            xs[x, 0] = jnp.zeros(xs.shape[2:], F32)

    @pl.when(me == N - 1)
    def _():
        for x in range(8):
            xb[x, 2:4] = jnp.zeros((2, W, W), F32)
        for x in range(2):
            xs[x, 1] = jnp.zeros(xs.shape[2:], F32)

    barrier = pltpu.get_barrier_semaphore()
    for d in [lax.rem(me + 1, N), lax.rem(me + N - 1, N)] + [partner(s) for s in range(steps)]:
        pl.semaphore_signal(barrier, inc=1, device_id=dev(d), device_id_type=MESH)

    def copy_to(x, small, side):
        buf, stage, a, b = (xs, sts, sssem, srsem) if small else (xb, st, ssem, rsem)
        at = side if small else pl.ds(2 * side, 2)
        return pltpu.make_async_remote_copy(
            stage.at[x, at], buf.at[x, at], a.at[x, side], b.at[x, side],
            device_id=dev(me + 1 - 2 * side), device_id_type=MESH)

    def start(x, small=False):
        @pl.when(up_ok)
        def _():
            copy_to(x, small, 0).start()

        @pl.when(down_ok)
        def _():
            copy_to(x, small, 1).start()

    def wait(x, small=False):
        @pl.when(up_ok)
        def _():
            copy_to(x, small, 0).wait_send()
            copy_to(x, small, 1).wait_recv()

        @pl.when(down_ok)
        def _():
            copy_to(x, small, 1).wait_send()
            copy_to(x, small, 0).wait_recv()

    count = meta[off["count"]]

    def live(b):
        return jnp.where(b < count, 1.0, 0.0).astype(F32)

    def one(b):
        return None

    def by(m, v):
        return v if m is None else v * m

    def tr(b, _):
        h0[b] = nodes[b].T
        return 0

    lax.fori_loop(0, nb, tr, 0)

    def stage_boundary(x, h):
        for j in range(2):
            st[x, j] = h[meta[off["boundary"] + j]]
            st[x, 2 + j] = h[meta[off["boundary"] + 2 + j]]

    stage_boundary(0, h0)
    pl.semaphore_wait(barrier, 2 + steps)
    start(0)

    def prep(l, _):
        WF[l, 0:256] = doubled(ws[l].T * 0.5)
        WF[l, 256:512] = doubled(wr[l].T * 0.5)
        WU[l] = doubled(wu[l].T)
        WUb[l] = doubled(wu[l])
        WSb[l] = doubled(ws[l])
        WRb[l] = doubled(wr[l])
        return 0

    lax.fori_loop(0, 3, prep, 0)
    for l in range(3):
        WE[l] = jnp.broadcast_to(we[l:l + 1, :] * 0.5, (W, W)).T
        BI[l] = jnp.broadcast_to(bias[l:l + 1, :] * 0.5, (W, W)).T
    acc[...] = jnp.zeros_like(acc)

    def project(l, nblk, h):
        g = min(4, nblk)

        def body(i, _):
            r = dot(WF[l], stacked(group(h, i, g)))
            o, v = halves(r[:256]), halves(r[256:])
            for j in range(g):
                own[g * i + j] = cols(o, j) + BI[l]
                recv[g * i + j] = cols(v, j)
            return 0

        lax.fori_loop(0, nblk // g, body, 0)

    def messages(l, nblk, k_, h, hn, D, agg, x, adj, ed, mask):
        v = halves(dot(WF[l, 256:512], stacked(group(xb.at[x], 0, 4))))
        for j in range(4):
            recv[nblk + j] = cols(v, j)

        def body(i, _):
            sums = []
            for j in range(2):
                b = 2 * i + j
                o = own[b]
                a = None
                for k in range(k_):
                    q = o + recv[meta[adj + b * k_ + k]] + WE[l] * ed[b, pl.ds(k, 1), :]
                    t = jnp.tanh(q)
                    qt = q * t
                    D[b * k_ + k] = (0.5 + 0.5 * t) * ((1.0 + q) - qt)
                    a = q + qt if a is None else a + (q + qt)
                agg[b] = a
                sums.append(a)
            u = halves(dot(WU[l], stacked(jnp.concatenate(sums, 1))))
            for j in range(2):
                b = 2 * i + j
                hn[b] = h[b] + by(mask(b), cols(u, j))
            return 0

        lax.fori_loop(0, nblk // 2, body, 0)

    def add_acc(row, value):
        acc[row:row + W] += value

    def backward(l, nblk, k_, h, go, D, agg, x, y, pre, ed, mask):
        base = 3 * W * l
        eacc[...] = jnp.zeros_like(eacc)
        bacc[...] = jnp.zeros_like(bacc)

        def body(i, _):
            bs = [2 * i, 2 * i + 1]
            us = stacked(jnp.concatenate([by(mask(b), go[b]) for b in bs], 1))
            ga = halves(dot(WUb[l], us))
            add_acc(base + 2 * W, quads(dot_t(stacked(group(agg, i, 2)), us)))
            sums = []
            for j, b in enumerate(bs):
                gj = cols(ga, j)
                s = e = None
                for k in range(k_):
                    m = gj * D[b * k_ + k]
                    G[b * k_ + k] = m
                    w = m * ed[b, pl.ds(k, 1), :]
                    s = m if s is None else s + m
                    e = w if e is None else e + w
                eacc[...] += e
                bacc[...] += s
                sums.append(s)
            ss = stacked(jnp.concatenate(sums, 1))
            add_acc(base, quads(dot_t(stacked(group(h, i, 2)), ss)))
            f = halves(dot(WSb[l], ss))
            for j, b in enumerate(bs):
                go[b] = go[b] + cols(f, j)
            return 0

        lax.fori_loop(0, nblk // 2, body, 0)
        small = 9 * W
        acc[small + l:small + l + 1] = jnp.sum(eacc[...].T, axis=0, keepdims=True)
        acc[small + 3 + l:small + 4 + l] = jnp.sum(bacc[...].T, axis=0, keepdims=True)

        def scan(j, run):
            run = run * meta[off[pre + "same"] + j].astype(F32) + G[meta[off[pre + "order"] + j]]
            S[j] = run
            return run

        lax.fori_loop(0, nblk * k_, scan, jnp.zeros((W, W), F32))

        def ext(e):
            return S[meta[off[pre + "end"] + e]] * meta[off[pre + "flag"] + e].astype(F32)

        xsx = stacked(jnp.concatenate([ext(nblk + j) for j in range(4)], 1))
        v = halves(dot(WRb[l], xsx))
        for j in range(2):
            st[y, 2 + j] = cols(v, j)
            st[y, j] = cols(v, 2 + j)
        start(y)
        add_acc(base + W, quads(dot_t(stacked(group(xb.at[x], 0, 4)), xsx)))
        g = min(4, nblk)

        def rest(i, _):
            es = stacked(jnp.concatenate([ext(g * i + j) for j in range(g)], 1))
            f = halves(dot(WRb[l], es))
            for j in range(g):
                go[g * i + j] = go[g * i + j] + cols(f, j)
            add_acc(base + W, quads(dot_t(stacked(group(h, i, g)), es)))
            return 0

        lax.fori_loop(0, nblk // g, rest, 0)
        wait(y)

    def returned(go, y, b):
        v = go[b]
        for j in range(2):
            v = v + xb[y, j] * jnp.where(meta[off["boundary"] + 2 + j] == b, 1.0, 0.0).astype(F32)
            v = v + xb[y, 2 + j] * jnp.where(meta[off["boundary"] + j] == b, 1.0, 0.0).astype(F32)
        return v

    project(0, nb, h0)

    def onehot(i, _):
        rows = lax.broadcasted_iota(jnp.int32, (W, n), 0) + i * W
        oh[pl.ds(pl.multiple_of(i * W, W), W), :] = jnp.where(rows == assign[...], 1.0, 0.0).astype(BF16)
        return 0

    lax.fori_loop(0, 3 * nc, onehot, 0)
    wait(0)
    messages(0, nb, K, h0, h1, D0, agg0, 0, off["adj"], edges, live)
    stage_boundary(1, h1)
    start(1)
    project(1, nb, h1)
    wait(1)
    messages(1, nb, K, h1, h2, D1, agg1, 1, off["adj"], edges, live)

    for b in range(nb):
        h2s[:, b * W:(b + 1) * W] = stacked(h2[b])

    def restricted(c):
        return halves(dot_t(h2s[...], oh[c * ncd:(c + 1) * ncd, :]))

    v = restricted(1)
    for j in range(nc):
        st[2, 2 + j] = cols(v, j)
    v = restricted(2)
    for j in range(nc):
        st[2, j] = cols(v, j)
    start(2)
    v = restricted(0)
    w8[...] = jnp.zeros_like(w8)
    w8[0:4] = wo[...]
    t8[...] = jnp.zeros_like(t8)
    t8[0:4] = targets[...]
    whi, wlo = split(w8[...])
    whi, wlo = whi.astype(F32), wlo.astype(F32)
    wd = jnp.concatenate([jnp.concatenate([whi, whi], 1), jnp.concatenate([wlo, wlo], 1)], 0).astype(BF16)
    fill = jnp.zeros((W - 16, W), F32)
    wt = jnp.concatenate([jnp.concatenate([whi, whi, fill], 0).T, jnp.concatenate([wlo, wlo, fill], 0).T], 0).astype(BF16)

    def rows16(x):
        hi, lo = split(x)
        return jnp.concatenate([hi.astype(F32), lo.astype(F32)], 0)

    wait(2)
    for j in range(nc):
        c0[j] = (cols(v, j) + xb[2, j] + xb[2, 2 + j]) * 0.125
        st[3, j] = c0[j]
        st[3, 2 + j] = c0[j]
    start(3)
    project(2, nc, c0)
    wait(3)
    messages(2, nc, KC, c0, c1, D2, agg2, 3, off["cadj"], cedges, one)

    c1s = stacked(group(c1, 0, nc))
    pc = halves(dot(wd, c1s))
    sts[0, 0] = pc
    sts[0, 1] = pc
    start(0, True)
    pred = halves(dot(wd, h2s[...])) + halves(dot(rows16(pc).astype(BF16), oh[0:ncd, :]))
    wait(0, True)
    pn = jnp.concatenate([rows16(xs[0, 0]), rows16(xs[0, 1])], 1).astype(BF16)
    pred = pred + halves(dot(pn, oh[ncd:3 * ncd, :]))
    err = jnp.where(lax.broadcasted_iota(jnp.int32, (8, n), 1) < count * W, pred - t8[...], 0.0)
    small = 9 * W
    e2 = err * err
    tot = e2[:, :W]
    for b in range(1, nb):
        tot = tot + cols(e2, b)
    acc[small + 10:small + 11] = jnp.broadcast_to(jnp.sum(tot).reshape(1, 1), (1, W))
    acc[small + 11:small + 12] = jnp.broadcast_to(count.astype(F32), (1, W))
    gp[...] = err * (2.0 / (4.0 * W * nb * N))
    g16 = rows16(gp[...])
    g16b = g16.astype(BF16)
    gq = halves(dot_t(g16b, oh[ncd:3 * ncd, :]))
    sts[1, 1] = gq[:, :ncd]
    sts[1, 0] = gq[:, ncd:]
    start(1, True)
    gq = halves(dot_t(g16b, oh[0:ncd, :]))
    go8 = quads(dot_t(g16b, h2s[...]))
    wait(1, True)
    gq = gq + xs[1, 0] + xs[1, 1]
    q16 = rows16(gq)
    go8 = go8 + quads(dot_t(q16.astype(BF16), c1s))
    acc[small + 6:small + 10] = go8[0:4]
    f = halves(dot(wt, jnp.concatenate([q16, jnp.zeros((W - 16, ncd), F32)], 0).astype(BF16)))
    for j in range(nc):
        gc[j] = cols(f, j)

    backward(2, nc, KC, c0, gc, D2, agg2, 3, 4, "c", cedges, one)
    for j in range(nc):
        v = (gc[j] + xb[4, j] + xb[4, 2 + j]) * 0.125
        st[5, j] = v
        st[5, 2 + j] = v
    start(5)
    gp128 = jnp.concatenate([g16, jnp.zeros((W - 16, n), F32)], 0).astype(BF16)
    f = halves(dot(wt, gp128))
    f = f + halves(dot(stacked(jnp.concatenate([st[5, j] for j in range(nc)], 1)), oh[0:ncd, :]))
    wait(5)
    f = f + halves(dot(stacked(group(xb.at[5], 0, 4)), oh[ncd:3 * ncd, :]))
    for b in range(nb):
        gr[b] = cols(f, b)

    backward(1, nb, K, h1, gr, D1, agg1, 1, 6, "", edges, live)

    def ret(b, _):
        gr[b] = returned(gr, 6, b)
        return 0

    lax.fori_loop(0, nb, ret, 0)
    backward(0, nb, K, h0, gr, D0, agg0, 0, 7, "", edges, live)

    lo = 0 * me
    size = R
    spot = 0
    for s in range(steps):
        size //= 2
        mine = (me // (1 << s)) % 2
        copy = pltpu.make_async_remote_copy(
            acc.at[pl.ds(pl.multiple_of(lo + (1 - mine) * size, 8), size)], rsb.at[pl.ds(spot, size)],
            assem.at[s], arsem.at[s], device_id=dev(partner(s)), device_id_type=MESH)
        copy.start()
        if s == 0:
            def fin(b, _):
                gr[b] = returned(gr, 7, b).T
                return 0

            lax.fori_loop(0, nb, fin, 0)
        copy.wait()
        lo = lo + mine * size
        keep = pl.ds(pl.multiple_of(lo, 8), size)
        acc[keep] += rsb[pl.ds(spot, size)]
        spot += size
    keep = pl.ds(pl.multiple_of(lo, 8), size)
    res[keep] = acc[keep]
    for s in range(steps - 1, -1, -1):
        mine = (me // (1 << s)) % 2
        part = res.at[pl.ds(pl.multiple_of(lo, 8), size)]
        copy = pltpu.make_async_remote_copy(
            part, part, assem.at[steps + s], arsem.at[steps + s], device_id=dev(partner(s)), device_id_type=MESH)
        copy.start()
        copy.wait()
        lo = lo - mine * size
        size *= 2

    total = res[small + 11:small + 12]
    ratio = (1.0 * nb * N) / total
    for l in range(3):
        gs_o[l] = res[3 * W * l:3 * W * l + W] * ratio
        gr_o[l] = res[3 * W * l + W:3 * W * l + 2 * W] * ratio
        gu_o[l] = res[3 * W * l + 2 * W:3 * W * l + 3 * W] * ratio
    ge_o[...] = res[small:small + 3] * ratio
    gb_o[...] = res[small + 3:small + 6] * ratio
    go_o[...] = res[small + 6:small + 10] * ratio
    loss_o[...] = res[small + 10:small + 11] / (4.0 * W * total)

    def out(b, _):
        dn[b] = gr[b] * ratio
        return 0

    lax.fori_loop(0, nb, out, 0)


def sort_info(adj, ext):
    a = adj.reshape(-1)
    m = a.shape[0]
    i = jnp.arange(m, dtype=jnp.int32)
    rank = jnp.sum(((a[None, :] < a[:, None]) | ((a[None, :] == a[:, None]) & (i[None, :] < i[:, None]))).astype(jnp.int32), 1)
    hit = rank[None, :] == i[:, None]
    order = jnp.sum(jnp.where(hit, i[None, :], 0), 1)
    value = jnp.sum(jnp.where(hit, a[None, :], 0), 1)
    before = jnp.sum(jnp.where(rank[None, :] == i[:, None] - 1, a[None, :], 0), 1)
    same = ((value == before) & (i > 0)).astype(jnp.int32)
    e = jnp.arange(ext, dtype=jnp.int32)
    end = jnp.maximum(jnp.sum((a[None, :] <= e[:, None]).astype(jnp.int32), 1) - 1, 0)
    flag = (jnp.sum((a[None, :] == e[:, None]).astype(jnp.int32), 1) > 0).astype(jnp.int32)
    return order, same, end, flag


def local(N, nodes, edges, adjacency, boundary, assign, coarse_adj, coarse_edges, counts, targets, ws, wr, wu, we, bias, wo):
    nb, K, _ = edges.shape
    nc, KC, _ = coarse_edges.shape
    n = nb * W
    ncd = nc * W
    steps = N.bit_length() - 1
    unit = 8 * N
    R = -(-(9 * W + 12) // unit) * unit
    order, same, end, flag = sort_info(adjacency, nb + 4)
    corder, csame, cend, cflag = sort_info(coarse_adj, 3 * nc)
    parts = {"adj": adjacency.reshape(-1), "boundary": boundary.reshape(-1), "count": counts, "cadj": coarse_adj.reshape(-1),
             "order": order, "same": same, "end": end, "flag": flag, "corder": corder, "csame": csame, "cend": cend, "cflag": cflag}
    off, at = {}, 0
    for name, value in parts.items():
        off[name] = at
        at += value.shape[0]
    meta = jnp.concatenate(list(parts.values()))
    vm = pl.BlockSpec(memory_space=pltpu.VMEM)
    blk = lambda m: pltpu.VMEM((m, W, W), F32)
    b16 = lambda *s: pltpu.VMEM(s, BF16)
    f32 = lambda *s: pltpu.VMEM(s, F32)
    sd = lambda *s: jax.ShapeDtypeStruct(s, F32)
    outs = pl.pallas_call(
        functools.partial(kernel, N, nb, nc, K, KC, R, off),
        out_shape=(sd(nb, W, W), sd(3, W, W), sd(3, W, W), sd(3, W, W), sd(3, W), sd(3, W), sd(4, W), sd(1, W)),
        in_specs=[pl.BlockSpec(memory_space=pltpu.SMEM)] + [vm] * 11,
        out_specs=(vm,) * 8,
        scratch_shapes=[
            blk(nb), blk(nb), blk(nb), blk(nc), blk(nc), blk(nb), blk(nb + 4),
            blk(nb * K), blk(nb * K), blk(nc * KC), blk(nb), blk(nb), blk(nc), blk(nb * K), blk(nb * K), blk(nb), blk(nc),
            b16(3 * ncd, n), b16(2 * W, n), b16(3, 512, 256), b16(3, 256, 256), b16(3, 256, 256), b16(3, 256, 256), b16(3, 256, 256),
            blk(3), blk(3), f32(W, W), f32(W, W), f32(8, 4, W, W), f32(8, 4, W, W), f32(2, 2, 8, ncd), f32(2, 2, 8, ncd),
            f32(8, n), f32(8, W), f32(8, n), f32(R, W), f32(R, W), f32(R, W),
            pltpu.SemaphoreType.DMA((8, 2)), pltpu.SemaphoreType.DMA((8, 2)), pltpu.SemaphoreType.DMA((2, 2)), pltpu.SemaphoreType.DMA((2, 2)),
            pltpu.SemaphoreType.DMA((2 * steps,)), pltpu.SemaphoreType.DMA((2 * steps,)),
        ],
        compiler_params=pltpu.CompilerParams(collective_id=0, has_side_effects=True, vmem_limit_bytes=56 * 1024 * 1024),
    )(meta, nodes.reshape(nb, W, W), edges, assign.reshape(1, n), coarse_edges, targets, ws, wr, wu, we, bias, wo)
    return (outs[7][0, :1], outs[0].reshape(n, W)) + outs[1:7]


def solution(mesh):
    both = ("groups", "dom")
    in_specs = (
        P(both, None), P(both, None, None), P(both, None), P(both, None), P(both), P(both, None), P(both, None, None), P(both),
        P(None, both), P(), P(), P(), P(), P(), P(),
    )
    out_specs = (
        P("groups"), P(both, None), P("groups", None, None), P("groups", None, None), P("groups", None, None),
        P("groups", None), P("groups", None), P("groups", None),
    )
    return jax.shard_map(functools.partial(local, mesh.shape["dom"]), mesh=mesh, in_specs=in_specs, out_specs=out_specs, check_vma=False)
```

time: 386 us -> 109 us (0.28); the launches traced: 380 us -> 109 us
  matrix products: 113 us -> 0 us
  Pallas kernels: 0 us -> 94.7 us
  blocking collectives: 67.3 us -> 0 us
  starting transfers between devices: 62.3 us -> 0 us
  waiting for transfers between devices: 54.7 us -> 0 us
  other arithmetic: 45.5 us -> 1.07 us
  between operations: 18.6 us -> 2.55 us
  local copies, waits for them, and re-layouts: 18 us -> 10.4 us
    dot_general x37 -> x0, matrix products: 113 us -> none  [the longest x3 17.3 us: layer_forward(): jnp.einsum('nkbh,hg->nkbg', neigh, w_r, precision=HIGH)]
    pallas_call x0 -> x1, Pallas kernels: none -> 94.7 us  [local(): pl.pallas_call(functools.partial(kernel, N, nb, nc, K, KC, R, off), out_s...]
    psum x2 -> x0, blocking collectives: 67.3 us -> none  [local(): merged = lax.psum(readout + cgrads + fine_grads[0] + fine_grads[1], 'dom')]
    ppermute x20 -> x0, starting transfers between devices: 62.2 us -> none  [passed_along(): lax.ppermute(value, axis, [(source, source + steps) for source in range(l...]
    psum x1 -> x0, waiting for transfers between devices: 51.2 us -> none  [local(): merged = lax.psum(readout + cgrads + fine_grads[0] + fine_grads[1], 'dom')]
    scatter-add x9 -> x0, other arithmetic: 29.4 us -> none  [the longest x3 19.7 us: layer_backward(): jnp.zeros((blocks + 2 * width,) + feats.shape[1:], jnp.float32).at[adj]]
    gather x7 -> x0, local copies, waits for them, and re-layouts: 11.1 us -> none  [the longest x3 6.17 us: layer_forward(): neigh = ext[adj]]
    unnamed x113 -> x28, local copies, waits for them, and re-layouts: 2.62 us -> 9.49 us
  transfers between devices with their start and end apart: 21 -> 0, of which waited for: 5 -> 0; matrix products, arithmetic and copies ran while one was open for 7% -> 0% of each run, Pallas kernels for 0% -> 0%
where the time goes in v1:
time: 109 us
  Pallas kernels  94.7 us (87%)
  local copies, waits for them, and re-layouts  10.4 us (10%)
  between operations  2.55 us (2%)
    pallas_call x1, Pallas kernels, local(): pl.pallas_call(functools.partial(kernel, N, nb, nc, K, KC, R, off), out_s...  94.7 us
    unnamed x28, local copies, waits for them, and re-layouts  9.49 us

profile of v1, /device:TPU:0, one launch (start us, length us, event | category | flops | bytes accessed | tf_op | source)
XLA Modules:
  0.0 108.7 jit_solution(9097320308027209051)
XLA Ops:
  1.3 0.0 copy-start.7
  1.3 0.7 copy-done.7
  2.0 0.1 reshape.52
  2.0 0.0 copy-start.8
  2.0 0.2 convert_reduce_fusion.5
  2.2 0.5 copy-done.8
  2.7 0.1 reshape.51
  2.8 0.2 select_reduce_fusion.3
  3.0 0.1 convert_reduce_fusion.3
  3.1 0.0 copy-start.3
  3.2 0.7 copy-done.3
  3.8 0.1 copy.25
  3.9 0.1 reshape.50
  4.0 0.2 convert_reduce_fusion
  4.2 0.2 select_reduce_fusion
  4.4 0.1 convert_reduce_fusion.1
  4.6 0.7 concatenate.3.meta
  5.2 94.7 %shard_map.206 = (f32[16,128,128]{2,1,0:T(8,128)}, f32[3,128,128]{2,1,0:T(8,128)}, f32[3,128,128]{2,1,0:T(8,128)}, f32[3,128,128]{2,1,0:T(8,128)}, f32[3,128]{1,...) custom-call(s32[273]{0:T(512)} %concatenate.3.meta, f32[16,128,128]{2,1,0:T(8,128)} %bitcast.5, ...), custom_call_target="tpu_custom_call" | custom-call | tf_op jit(solution)/shard_map/pallas_call | solution.py:480
  100.0 0.0 copy-start.9
  100.0 0.7 copy-done.9
  100.7 0.0 copy-start.2
  100.7 2.3 %copy.36 = f32[2048,128]{1,0:T(8,128)} copy(f32[2048,128]{1,0:T(8,128)} %bitcast.6) | data formatting | bytes 2097152
  103.0 0.0 copy-done.2
  103.0 0.0 copy-start.1
  103.0 0.7 copy.37
  103.7 0.3 copy-done.1
  104.0 0.0 copy-start
  104.0 0.7 copy.38
  104.7 0.3 copy-done
  105.0 0.0 copy-start.6
  105.0 0.7 copy.39
  105.7 0.0 copy-done.6
  105.7 0.0 copy-start.5
  105.7 0.6 copy.40
  106.2 0.1 copy-done.5
  106.4 0.0 copy-start.4
  106.4 0.6 copy.41
  106.9 0.1 copy-done.4
  107.0 0.6 copy.42
  (8 shorter events, 0.0 us)
Async XLA Ops:
  1.3 0.7 copy-start.7
  2.0 0.7 copy-start.8
  3.1 0.7 copy-start.3
  100.0 0.7 copy-start.9
  100.7 2.3 %copy-start.2 = (f32[3,128,128]{2,1,0:T(8,128)S(1)}, f32[3,128,128]{2,1,0:T(8,128)}, u32[]{:S(2)}) copy-start(f32[3,128,128]{2,1,0:T(8,128)} %get-tuple-element.44) | copy-start | bytes 589828
  103.0 1.0 copy-start.1
  104.0 1.0 copy-start
  105.0 0.7 copy-start.6
  105.7 0.7 copy-start.5
  106.4 0.7 copy-start.4

commit v2 on v1

--- a/solution.py
+++ b/solution.py
@@ -53,9 +53,9 @@
     return x[:, j * W:(j + 1) * W]
 
 
-def kernel(N, nb, nc, K, KC, R, off,
+def kernel(N, nb, nc, K, KC, RA, RB, off,
            meta, nodes, edges, assign, cedges, targets, ws, wr, wu, we, bias, wo,
-           dn, gs_o, gr_o, gu_o, ge_o, gb_o, go_o, loss_o,
+           dn, res_o,
            h0, h1, h2, c0, c1, own, recv, D0, D1, D2, agg0, agg1, agg2, G, S, gr, gc,
            oh, h2s, WF, WU, WUb, WSb, WRb, WE, BI, eacc, bacc, xb, st, xs, sts, t8, w8, gp, acc, rsb, res,
            ssem, rsem, sssem, srsem, assem, arsem):
@@ -172,7 +172,7 @@
                 recv[g * i + j] = cols(v, j)
             return 0
 
-        lax.fori_loop(0, nblk // g, body, 0)
+        lax.fori_loop(0, nblk // g, body, 0, unroll=True)
 
     def messages(l, nblk, k_, h, hn, D, agg, x, adj, ed, mask):
         v = halves(dot(WF[l, 256:512], stacked(group(xb.at[x], 0, 4))))
@@ -199,13 +199,18 @@
                 hn[b] = h[b] + by(mask(b), cols(u, j))
             return 0
 
-        lax.fori_loop(0, nblk // 2, body, 0)
+        lax.fori_loop(0, nblk // 2, body, 0, unroll=2)
+
+    base_of = {0: RA, 1: 0, 2: 3 * W}
+    ge_of = {0: RA + 3 * W, 1: 6 * W, 2: 6 * W + 1}
+    gb_of = {0: RA + 3 * W + 1, 1: 6 * W + 2, 2: 6 * W + 3}
 
     def add_acc(row, value):
         acc[row:row + W] += value
 
-    def backward(l, nblk, k_, h, go, D, agg, x, y, pre, ed, mask):
-        base = 3 * W * l
+    def backward(l, nblk, k_, h, go, D, agg, x, y, pre, ed, mask, hook=None):
+        base = base_of[l]
+        hook = hook or (lambda: None)
         eacc[...] = jnp.zeros_like(eacc)
         bacc[...] = jnp.zeros_like(bacc)
 
@@ -234,17 +239,25 @@
                 go[b] = go[b] + cols(f, j)
             return 0
 
-        lax.fori_loop(0, nblk // 2, body, 0)
-        small = 9 * W
-        acc[small + l:small + l + 1] = jnp.sum(eacc[...].T, axis=0, keepdims=True)
-        acc[small + 3 + l:small + 4 + l] = jnp.sum(bacc[...].T, axis=0, keepdims=True)
+        hook()
+        pairs = nblk // 2
+        lax.fori_loop(0, pairs // 2, body, 0, unroll=2)
+        hook()
+        lax.fori_loop(pairs // 2, pairs, body, 0, unroll=2)
+        hook()
+        acc[ge_of[l]:ge_of[l] + 1] = jnp.sum(eacc[...].T, axis=0, keepdims=True)
+        acc[gb_of[l]:gb_of[l] + 1] = jnp.sum(bacc[...].T, axis=0, keepdims=True)
 
         def scan(j, run):
             run = run * meta[off[pre + "same"] + j].astype(F32) + G[meta[off[pre + "order"] + j]]
             S[j] = run
             return run
 
-        lax.fori_loop(0, nblk * k_, scan, jnp.zeros((W, W), F32))
+        half = nblk * k_ // 2
+        run = lax.fori_loop(0, half, scan, jnp.zeros((W, W), F32), unroll=8)
+        hook()
+        lax.fori_loop(half, nblk * k_, scan, run, unroll=8)
+        hook()
 
         def ext(e):
             return S[meta[off[pre + "end"] + e]] * meta[off[pre + "flag"] + e].astype(F32)
@@ -255,6 +268,7 @@
             st[y, 2 + j] = cols(v, j)
             st[y, j] = cols(v, 2 + j)
         start(y)
+        hook()
         add_acc(base + W, quads(dot_t(stacked(group(xb.at[x], 0, 4)), xsx)))
         g = min(4, nblk)
 
@@ -266,7 +280,8 @@
             add_acc(base + W, quads(dot_t(stacked(group(h, i, g)), es)))
             return 0
 
-        lax.fori_loop(0, nblk // g, rest, 0)
+        lax.fori_loop(0, nblk // g, rest, 0, unroll=True)
+        hook()
         wait(y)
 
     def returned(go, y, b):
@@ -340,13 +355,13 @@
     pn = jnp.concatenate([rows16(xs[0, 0]), rows16(xs[0, 1])], 1).astype(BF16)
     pred = pred + halves(dot(pn, oh[ncd:3 * ncd, :]))
     err = jnp.where(lax.broadcasted_iota(jnp.int32, (8, n), 1) < count * W, pred - t8[...], 0.0)
-    small = 9 * W
+    small = 6 * W
     e2 = err * err
     tot = e2[:, :W]
     for b in range(1, nb):
         tot = tot + cols(e2, b)
-    acc[small + 10:small + 11] = jnp.broadcast_to(jnp.sum(tot).reshape(1, 1), (1, W))
-    acc[small + 11:small + 12] = jnp.broadcast_to(count.astype(F32), (1, W))
+    acc[small + 8:small + 9] = jnp.broadcast_to(jnp.sum(tot).reshape(1, 1), (1, W))
+    acc[small + 9:small + 10] = jnp.broadcast_to(count.astype(F32), (1, W))
     gp[...] = err * (2.0 / (4.0 * W * nb * N))
     g16 = rows16(gp[...])
     g16b = g16.astype(BF16)
@@ -360,7 +375,7 @@
     gq = gq + xs[1, 0] + xs[1, 1]
     q16 = rows16(gq)
     go8 = go8 + quads(dot_t(q16.astype(BF16), c1s))
-    acc[small + 6:small + 10] = go8[0:4]
+    acc[small + 4:small + 8] = go8[0:4]
     f = halves(dot(wt, jnp.concatenate([q16, jnp.zeros((W - 16, ncd), F32)], 0).astype(BF16)))
     for j in range(nc):
         gc[j] = cols(f, j)
@@ -386,51 +401,64 @@
         return 0
 
     lax.fori_loop(0, nb, ret, 0)
-    backward(0, nb, K, h0, gr, D0, agg0, 0, 7, "", edges, live)
-
-    lo = 0 * me
-    size = R
-    spot = 0
-    for s in range(steps):
-        size //= 2
-        mine = (me // (1 << s)) % 2
-        copy = pltpu.make_async_remote_copy(
-            acc.at[pl.ds(pl.multiple_of(lo + (1 - mine) * size, 8), size)], rsb.at[pl.ds(spot, size)],
-            assem.at[s], arsem.at[s], device_id=dev(partner(s)), device_id_type=MESH)
-        copy.start()
-        if s == 0:
-            def fin(b, _):
-                gr[b] = returned(gr, 7, b).T
-                return 0
-
-            lax.fori_loop(0, nb, fin, 0)
-        copy.wait()
-        lo = lo + mine * size
-        keep = pl.ds(pl.multiple_of(lo, 8), size)
-        acc[keep] += rsb[pl.ds(spot, size)]
-        spot += size
-    keep = pl.ds(pl.multiple_of(lo, 8), size)
-    res[keep] = acc[keep]
-    for s in range(steps - 1, -1, -1):
-        mine = (me // (1 << s)) % 2
-        part = res.at[pl.ds(pl.multiple_of(lo, 8), size)]
-        copy = pltpu.make_async_remote_copy(
-            part, part, assem.at[steps + s], arsem.at[steps + s], device_id=dev(partner(s)), device_id_type=MESH)
-        copy.start()
-        copy.wait()
-        lo = lo - mine * size
-        size *= 2
-
-    total = res[small + 11:small + 12]
+
+    def summed(base, rows, q):
+        lo, size, spot = base + 0 * me, rows, base
+        for s in range(steps):
+            size //= 2
+            mine = (me // (1 << s)) % 2
+            copy = pltpu.make_async_remote_copy(
+                acc.at[pl.ds(pl.multiple_of(lo + (1 - mine) * size, 8), size)], rsb.at[pl.ds(spot, size)],
+                assem.at[q + s], arsem.at[q + s], device_id=dev(partner(s)), device_id_type=MESH)
+            copy.start()
+            yield
+            copy.wait()
+            lo = lo + mine * size
+            keep = pl.ds(pl.multiple_of(lo, 8), size)
+            acc[keep] += rsb[pl.ds(spot, size)]
+            spot += size
+        res[keep] = acc[keep]
+        for s in range(steps - 1, -1, -1):
+            mine = (me // (1 << s)) % 2
+            part = res.at[pl.ds(pl.multiple_of(lo, 8), size)]
+            copy = pltpu.make_async_remote_copy(
+                part, part, assem.at[q + steps + s], arsem.at[q + steps + s], device_id=dev(partner(s)), device_id_type=MESH)
+            copy.start()
+            yield
+            copy.wait()
+            lo = lo - mine * size
+            size *= 2
+
+    early = summed(0, RA, 0)
+    backward(0, nb, K, h0, gr, D0, agg0, 0, 7, "", edges, live, lambda: next(early, None))
+    late = summed(RA, RB, 2 * steps)
+    next(late)
+
+    def fin(b, _):
+        dn[b] = returned(gr, 7, b).T
+        return 0
+
+    lax.fori_loop(0, nb, fin, 0)
+    for _ in range(2 * steps):
+        next(early, None)
+        next(late, None)
+    res_o[...] = res[...]
+
+
+def finish(nb, N, RA, gr, res, dn, gs_o, gr_o, gu_o, ge_o, gb_o, go_o, loss_o):
+    small = 6 * W
+    total = res[small + 9:small + 10]
     ratio = (1.0 * nb * N) / total
-    for l in range(3):
-        gs_o[l] = res[3 * W * l:3 * W * l + W] * ratio
-        gr_o[l] = res[3 * W * l + W:3 * W * l + 2 * W] * ratio
-        gu_o[l] = res[3 * W * l + 2 * W:3 * W * l + 3 * W] * ratio
-    ge_o[...] = res[small:small + 3] * ratio
-    gb_o[...] = res[small + 3:small + 6] * ratio
-    go_o[...] = res[small + 6:small + 10] * ratio
-    loss_o[...] = res[small + 10:small + 11] / (4.0 * W * total)
+    for l, base in ((0, RA), (1, 0), (2, 3 * W)):
+        gs_o[l] = res[base:base + W] * ratio
+        gr_o[l] = res[base + W:base + 2 * W] * ratio
+        gu_o[l] = res[base + 2 * W:base + 3 * W] * ratio
+    ge_o[0:1] = res[RA + 3 * W:RA + 3 * W + 1] * ratio
+    ge_o[1:3] = res[small:small + 2] * ratio
+    gb_o[0:1] = res[RA + 3 * W + 1:RA + 3 * W + 2] * ratio
+    gb_o[1:3] = res[small + 2:small + 4] * ratio
+    go_o[...] = res[small + 4:small + 8] * ratio
+    loss_o[...] = res[small + 8:small + 9] / (4.0 * W * total)
 
     def out(b, _):
         dn[b] = gr[b] * ratio
@@ -462,7 +490,9 @@
     ncd = nc * W
     steps = N.bit_length() - 1
     unit = 8 * N
-    R = -(-(9 * W + 12) // unit) * unit
+    RA = -(-(6 * W + 10) // unit) * unit
+    RB = -(-(3 * W + 2) // unit) * unit
+    R = RA + RB
     order, same, end, flag = sort_info(adjacency, nb + 4)
     corder, csame, cend, cflag = sort_info(coarse_adj, 3 * nc)
     parts = {"adj": adjacency.reshape(-1), "boundary": boundary.reshape(-1), "count": counts, "cadj": coarse_adj.reshape(-1),
@@ -477,11 +507,11 @@
     b16 = lambda *s: pltpu.VMEM(s, BF16)
     f32 = lambda *s: pltpu.VMEM(s, F32)
     sd = lambda *s: jax.ShapeDtypeStruct(s, F32)
-    outs = pl.pallas_call(
-        functools.partial(kernel, N, nb, nc, K, KC, R, off),
-        out_shape=(sd(nb, W, W), sd(3, W, W), sd(3, W, W), sd(3, W, W), sd(3, W), sd(3, W), sd(4, W), sd(1, W)),
+    carried, sums = pl.pallas_call(
+        functools.partial(kernel, N, nb, nc, K, KC, RA, RB, off),
+        out_shape=(sd(nb, W, W), sd(R, W)),
         in_specs=[pl.BlockSpec(memory_space=pltpu.SMEM)] + [vm] * 11,
-        out_specs=(vm,) * 8,
+        out_specs=(vm,) * 2,
         scratch_shapes=[
             blk(nb), blk(nb), blk(nb), blk(nc), blk(nc), blk(nb), blk(nb + 4),
             blk(nb * K), blk(nb * K), blk(nc * KC), blk(nb), blk(nb), blk(nc), blk(nb * K), blk(nb * K), blk(nb), blk(nc),
@@ -489,10 +519,16 @@
             blk(3), blk(3), f32(W, W), f32(W, W), f32(8, 4, W, W), f32(8, 4, W, W), f32(2, 2, 8, ncd), f32(2, 2, 8, ncd),
             f32(8, n), f32(8, W), f32(8, n), f32(R, W), f32(R, W), f32(R, W),
             pltpu.SemaphoreType.DMA((8, 2)), pltpu.SemaphoreType.DMA((8, 2)), pltpu.SemaphoreType.DMA((2, 2)), pltpu.SemaphoreType.DMA((2, 2)),
-            pltpu.SemaphoreType.DMA((2 * steps,)), pltpu.SemaphoreType.DMA((2 * steps,)),
+            pltpu.SemaphoreType.DMA((4 * steps,)), pltpu.SemaphoreType.DMA((4 * steps,)),
         ],
         compiler_params=pltpu.CompilerParams(collective_id=0, has_side_effects=True, vmem_limit_bytes=56 * 1024 * 1024),
     )(meta, nodes.reshape(nb, W, W), edges, assign.reshape(1, n), coarse_edges, targets, ws, wr, wu, we, bias, wo)
+    outs = pl.pallas_call(
+        functools.partial(finish, nb, N, RA),
+        out_shape=(sd(nb, W, W), sd(3, W, W), sd(3, W, W), sd(3, W, W), sd(3, W), sd(3, W), sd(4, W), sd(1, W)),
+        in_specs=[vm] * 2,
+        out_specs=(vm,) * 8,
+    )(carried, sums)
     return (outs[7][0, :1], outs[0].reshape(n, W)) + outs[1:7]
 
 

time: 109 us -> 108 us (level)
  local copies, waits for them, and re-layouts: 10.4 us -> 2.83 us
  Pallas kernels: 94.7 us -> 102 us
  between operations: 2.55 us -> 1.35 us
    unnamed x28 -> x7, local copies, waits for them, and re-layouts: 9.49 us -> 1.91 us
    pallas_call x1 -> x2, Pallas kernels: 94.7 us -> 102 us  [the longest x1 99.4 us: local(): pl.pallas_call(functools.partial(kernel, N, nb, nc, K, KC, RA, RB, off),...]
where the time goes in v2:
time: 108 us; the launch traced here: 107 us
  Pallas kernels  102 us (94%)
  local copies, waits for them, and re-layouts  2.83 us (3%)
  between operations  1.35 us (1%)
    pallas_call x1, Pallas kernels, local(): pl.pallas_call(functools.partial(kernel, N, nb, nc, K, KC, RA, RB, off),...  99.4 us
    pallas_call x1, Pallas kernels, local(): pl.pallas_call(functools.partial(finish, nb, N, RA), out_shape=(sd(nb, W,...  2.75 us

profile of v2, /device:TPU:0, one launch (start us, length us, event | category | flops | bytes accessed | tf_op | source)
XLA Modules:
  0.0 107.5 jit_solution(8949677172256456167)
XLA Ops:
  1.3 0.0 copy-start.1
  1.3 0.7 copy-done.1
  2.0 0.1 reshape.52
  2.0 0.0 copy-start.2
  2.0 0.2 convert_reduce_fusion.5
  2.2 0.5 copy-done.2
  2.7 0.1 reshape.51
  2.8 0.2 select_reduce_fusion.3
  3.0 0.1 convert_reduce_fusion.3
  3.2 0.0 copy-start
  3.2 0.7 copy-done
  3.8 0.1 copy.25
  3.9 0.1 reshape.50
  4.0 0.2 convert_reduce_fusion
  4.2 0.2 select_reduce_fusion
  4.4 0.1 convert_reduce_fusion.1
  4.6 0.7 concatenate.3.meta
  5.2 99.4 %shard_map.206 = (f32[16,128,128]{2,1,0:T(8,128)}, f32[1408,128]{1,0:T(8,128)}) custom-call(s32[273]{0:T(512)} %concatenate.3.meta, f32[16,128,128]{2,1,0:T(8,128)} %bitcast.5, f32[16,4,128]{2,1,0:T(4,128)} %edges.1, s32[1,2048]{1,0:T(1,128)} %bitcast.6, f32[2,4,128]{2,1,0:T(4,128)} %cedges.1, f32[4,2048]{1,0:T(4,128)} %targets.1, f32[3,128,128]{2,1,0:T(8,128)} %ws.1, ...), custom_call_target="tpu_custom_call" | custom-call | tf_op jit(solution)/shard_map/pallas_call | solution.py:510
  104.7 2.7 %shard_map.207 = (f32[16,128,128]{2,1,0:T(8,128)}, f32[3,128,128]{2,1,0:T(8,128)}, f32[3,128,128]{2,1,0:T(8,128)}, f32[3,128,128]{2,1,0:T(8,128)}, f32[3,128]{1,...) custom-call(f32[16,128,128]{2,1,0:T(8,128)} %get-tuple-element.18.gr, ...), custom_call_target="tpu_custom_call" | custom-call | tf_op jit(solution)/shard_map/pallas_call | solution.py:526
  (8 shorter events, 0.0 us)
Async XLA Ops:
  1.3 0.7 copy-start.1
  2.0 0.7 copy-start.2
  3.2 0.7 copy-start

commit v3 on v2

--- a/solution.py
+++ b/solution.py
@@ -430,7 +430,8 @@
             size *= 2
 
     early = summed(0, RA, 0)
-    backward(0, nb, K, h0, gr, D0, agg0, 0, 7, "", edges, live, lambda: next(early, None))
+    calls = iter(range(99))
+    backward(0, nb, K, h0, gr, D0, agg0, 0, 7, "", edges, live, lambda: next(early, None) if next(calls) in (0, 2, 6) else None)
     late = summed(RA, RB, 2 * steps)
     next(late)
 
@@ -440,8 +441,8 @@
 
     lax.fori_loop(0, nb, fin, 0)
     for _ in range(2 * steps):
+        next(late, None)
         next(early, None)
-        next(late, None)
     res_o[...] = res[...]
 
 

time: 108 us -> 95.1 us (0.88)
  Pallas kernels: 102 us -> 89.6 us
    pallas_call x1, Pallas kernels: 99.4 us -> 86.8 us  [local(): pl.pallas_call(functools.partial(kernel, N, nb, nc, K, KC, RA, RB, off),...]
where the time goes in v3:
time: 95.1 us; the launch traced here: 94.8 us
  Pallas kernels  89.6 us (94%)
  local copies, waits for them, and re-layouts  2.83 us (3%)
  between operations  1.35 us (1%)
  other arithmetic  1.07 us (1%)
    pallas_call x1, Pallas kernels, local(): pl.pallas_call(functools.partial(kernel, N, nb, nc, K, KC, RA, RB, off),...  86.8 us
    pallas_call x1, Pallas kernels, local(): pl.pallas_call(functools.partial(finish, nb, N, RA), out_shape=(sd(nb, W,...  2.75 us
    unnamed x7, local copies, waits for them, and re-layouts  1.91 us

profile of v3, /device:TPU:0, one launch (start us, length us, event | category | flops | bytes accessed | tf_op | source)
XLA Modules:
  0.0 94.8 jit_solution(13665957838640662145)
XLA Ops:
  1.3 0.0 copy-start.1
  1.3 0.7 copy-done.1
  2.0 0.1 reshape.52
  2.0 0.0 copy-start.2
  2.0 0.2 convert_reduce_fusion.5
  2.2 0.5 copy-done.2
  2.7 0.1 reshape.51
  2.8 0.2 select_reduce_fusion.3
  3.0 0.1 convert_reduce_fusion.3
  3.2 0.0 copy-start
  3.2 0.7 copy-done
  3.8 0.1 copy.25
  3.9 0.1 reshape.50
  4.0 0.2 convert_reduce_fusion
  4.2 0.2 select_reduce_fusion
  4.4 0.1 convert_reduce_fusion.1
  4.6 0.7 concatenate.3.meta
  5.2 86.8 %shard_map.206 = (f32[16,128,128]{2,1,0:T(8,128)}, f32[1408,128]{1,0:T(8,128)}) custom-call(s32[273]{0:T(512)} %concatenate.3.meta, f32[16,128,128]{2,1,0:T(8,128)} %bitcast.5, f32[16,4,128]{2,1,0:T(4,128)} %edges.1, s32[1,2048]{1,0:T(1,128)} %bitcast.6, f32[2,4,128]{2,1,0:T(4,128)} %cedges.1, f32[4,2048]{1,0:T(4,128)} %targets.1, f32[3,128,128]{2,1,0:T(8,128)} %ws.1, ...), custom_call_target="tpu_custom_call" | custom-call | tf_op jit(solution)/shard_map/pallas_call | solution.py:511
  92.1 2.7 %shard_map.207 = (f32[16,128,128]{2,1,0:T(8,128)}, f32[3,128,128]{2,1,0:T(8,128)}, f32[3,128,128]{2,1,0:T(8,128)}, f32[3,128,128]{2,1,0:T(8,128)}, f32[3,128]{1,...) custom-call(f32[16,128,128]{2,1,0:T(8,128)} %get-tuple-element.18.gr, ...), custom_call_target="tpu_custom_call" | custom-call | tf_op jit(solution)/shard_map/pallas_call | solution.py:527
  (8 shorter events, 0.0 us)
Async XLA Ops:
  1.3 0.7 copy-start.1
  2.0 0.7 copy-start.2
  3.2 0.7 copy-start
